TPU v7x, 32 devices: a whole 2x2x4 slice. The times are simulated.
32 devices in a mesh: gx: 4 (over y, x), gy: 8 (over z, core).
Axes of the slice: x: 2, y: 2, z: 4, core: 2. Of those that a mesh axis runs over, the one named last changes fastest.
Arguments:
- momentum_dist: float32 [19, 32, 128, 512], P(None, 'gx', 'gy'), may hold values from 0.2 to 0.8
- order_dist: float32 [19, 32, 128, 512], P(None, 'gx', 'gy'), may hold values from -0.25 to 0.25
- offsets: int32 [4], replicated, may hold values from 64 to 79, as said below
Outputs:
- next_momentum: float32 [19, 32, 128, 512], P(None, 'gx', 'gy')
- next_order: float32 [19, 32, 128, 512], P(None, 'gx', 'gy')
Inputs may be any that keep to these rules, and one draw needn't show every extreme that they name: Every offsets[k] lies from 64 to 79; offsets[0] is 64 and offsets[3] is 79.
All inputs are finite; a program needn't handle non-finite values.
Results may differ from a plain program's by a relative error of at most 0.00002.
Values sent between devices are 32-bit elements; how exact they have to be, the bound alone decides.
No kernel may reach another device: no remote copies, remote signals or barrier semaphores. Data moves between devices by JAX's collectives and lax.ppermute only.
A program may use at most 128 MiB of HBM per device.

v0:
```python
import functools

import jax
import jax.numpy as jnp
from jax import lax
from jax.experimental import pallas as pl
from jax.experimental.pallas import tpu as pltpu
from jax.sharding import PartitionSpec as P

lattice_velocity = [
    (0, 0, 0),
    (1, 0, 0),
    (-1, 0, 0),
    (0, 1, 0),
    (0, -1, 0),
    (0, 0, 1),
    (0, 0, -1),
    (1, 1, 0),
    (-1, -1, 0),
    (1, -1, 0),
    (-1, 1, 0),
    (1, 0, 1),
    (-1, 0, -1),
    (1, 0, -1),
    (-1, 0, 1),
    (0, 1, 1),
    (0, -1, -1),
    (0, 1, -1),
    (0, -1, 1),
]
lattice_weight = [1.0 / 3.0] + [1.0 / 18.0] * 6 + [1.0 / 36.0] * 12
plane_speed = 0.04
rising = [1, 7, 9, 11, 13]
falling = [2, 8, 10, 12, 14]
north_going = [i for i in range(19) if lattice_velocity[i][1] == 1]
south_going = [i for i in range(19) if lattice_velocity[i][1] == -1]
f32 = jnp.float32
VMEM = pltpu.VMEM
LANES = 128


def z_moved(value, step):
    if step == 0:
        return value
    return pltpu.roll(value, step % value.shape[-1], value.ndim - 1)


def spec_of(space):
    return pl.BlockSpec(memory_space=space)


def params(limit):
    return pltpu.CompilerParams(vmem_limit_bytes=limit)


def along(parts, c):
    total = None
    for sign, part in zip(c, parts):
        if sign == 0:
            continue
        if total is None:
            total = part if sign > 0 else -part
        else:
            total = total + part if sign > 0 else total - part
    return total


def signed_sum(load, axis):
    ups = [i for i in range(19) if lattice_velocity[i][axis] == 1]
    downs = [i for i in range(19) if lattice_velocity[i][axis] == -1]
    total = load(ups[0]) - load(downs[0])
    for i, j in zip(ups[1:], downs[1:]):
        total = total + (load(i) - load(j))
    return total


def moments_of(load):
    rho = load(0)
    for i in range(1, 19):
        rho = rho + load(i)
    return [rho] + [signed_sum(load, axis) for axis in range(3)]


class Site:
    def __init__(self, moments, phi, minus, plus, south, north):
        rho, momentum = moments[0], moments[1:]
        lower, upper = z_moved(phi, 1), z_moved(phi, -1)
        lap = (plus + minus) + (north + south) + (upper + lower) - 6.0 * phi
        mu = phi * (0.0625 * (phi * phi) - 0.0625) - 0.04 * lap
        half_mu = 0.5 * mu
        force = [half_mu * (plus - minus), half_mu * (north - south), half_mu * (upper - lower)]
        inverse = 1.0 / rho
        u = [(j + 0.5 * k) * inverse for j, k in zip(momentum, force)]
        uu = u[0] * u[0] + u[1] * u[1] + u[2] * u[2]
        uf = u[0] * force[0] + u[1] * force[1] + u[2] * force[2]
        self.rho, self.phi, self.mu, self.u, self.force, self.uu = rho, phi, mu, u, force, uu
        self.r = 1.25 * rho
        self.k = self.r * (1.0 - 1.5 * uu) - 1.125 * uf
        self.g_scale = phi * (1.0 / 0.9)
        self.g_base = (3.0 / 0.9) * mu - 1.5 * (self.g_scale * uu)

    def pair_f(self, i):
        p, q = along(self.u, lattice_velocity[i]), along(self.force, lattice_velocity[i])
        w = lattice_weight[i]
        rp = self.r * p
        even = w * (self.k + p * (4.5 * rp + 3.375 * q))
        odd = (3.0 * w) * rp + (1.125 * w) * q
        return even, odd

    def pair_g(self, i):
        p = along(self.u, lattice_velocity[i])
        w = lattice_weight[i]
        gp = self.g_scale * p
        return w * (self.g_base + 4.5 * (gp * p)), (3.0 * w) * gp

    def jump(self, i, delta):
        cy = lattice_velocity[i][1]
        uy = self.u[1]
        if cy == 0:
            return delta * (-3.0 * uy) - (1.5 * delta * delta)
        p = along(self.u, lattice_velocity[i])
        return delta * (3.0 * cy + (9.0 * cy) * p - 3.0 * uy) + (3.0 * delta * delta)


class Shear:
    def __init__(self, raw, wide, rows):
        self.raw, self.wide, self.rows = raw, wide, rows

    def clear(self):
        self.raw[...] = jnp.zeros_like(self.raw)
        self.wide[...] = jnp.zeros_like(self.wide)

    def put(self, value, up, near, far):
        n = self.rows
        for k in range(self.raw.shape[0]):
            self.raw[k, 8 : 8 + n] = value[:, LANES * k : LANES * k + LANES]
        for k in range(self.raw.shape[0]):
            if up:
                self.wide[k, n : n + n + 8] = (
                    near * self.raw[k, 0 : n + 8] + far * self.raw[k, 1 : n + 9]
                )
            else:
                self.wide[k, n + 8 : n + n + 16] = (
                    near * self.raw[k, 7 : n + 15] + far * self.raw[k, 8 : n + 16]
                )

    def add_row(self, at, row):
        for k in range(self.raw.shape[0]):
            lanes = slice(LANES * k, LANES * k + LANES)
            self.wide[k, at : at + 1] = self.wide[k, at : at + 1] + row[:, lanes]

    def take(self, up, block, rest, cy, ref, j):
        n = self.rows
        if up:
            start = (n + 8 if block == 0 else 8) + rest - cy
        else:
            start = (n + 8 if block == 0 else n + n + 8) - rest - cy
        for k in range(self.raw.shape[0]):
            ref[j, 0:n, LANES * k : LANES * k + LANES] = self.wide[k, pl.ds(start, n)]


def plane_at(column, count_x):
    per_plane = count_x // 4
    is_plane = lax.rem(column, per_plane) == 0
    return is_plane, lax.rem(lax.div(column, per_plane), 4)


class Planes:
    def __init__(self, rests, count_x):
        self.up_rest, self.low_rest = rests
        self.odd = lax.rem(lax.axis_index("gy"), 2) == 1
        a = lax.axis_index("gx")

        def part_of(column):
            is_plane, plane = plane_at(column, count_x)
            return is_plane, (2.0 * plane.astype(f32) + 1.0) * 0.125

        up_is, up_part = part_of(lax.rem(a + 1, count_x))
        low_is, low_part = part_of(a)
        self.up_near = jnp.where(up_is, 1.0 - up_part, 1.0)
        self.up_far = jnp.where(up_is, up_part, 0.0)
        self.low_near = jnp.where(low_is, low_part, 0.0)
        self.low_far = jnp.where(low_is, 1.0 - low_part, 1.0)
        self.up_jump = jnp.where(up_is, -plane_speed, 0.0)
        self.low_jump = jnp.where(low_is, plane_speed, 0.0)


def order_sum(load):
    total = load(0)
    for i in range(1, 19):
        total = total + load(i)
    return total


def phi_kernel(f_ref, g_ref, top, bottom, phi_ref, to_north, to_south, gbuf, fbuf, sems):
    layers, rows = phi_ref.shape[0], phi_ref.shape[1]
    faces = (layers - 1, 0)
    f_copies = [
        pltpu.make_async_copy(f_ref.at[:, x], fbuf.at[:, s], sems.at[layers + s])
        for s, x in enumerate(faces)
    ]
    g_copies = [
        pltpu.make_async_copy(g_ref.at[:, x], gbuf.at[:, x], sems.at[x]) for x in range(layers)
    ]
    for copy in f_copies + g_copies:
        copy.start()
    phi_ref[layers - 1] = top[...]
    phi_ref[0] = bottom[...]
    edges = ((to_north, rows - 1, rows - 2, (7, 10)), (to_south, 0, 1, (9, 8)))
    for s, x in enumerate(faces):
        f_copies[s].wait()
        for out, edge, inner, chosen in edges:
            out[layers + s : layers + s + 1] = phi_ref[x, inner : inner + 1]
            at = layers + 2 + 6 * s
            out[at : at + 1] = fbuf[chosen[s], s, edge : edge + 1]
            for k, part in enumerate(moments_of(lambda i: fbuf[i, s, edge : edge + 1])):
                out[at + 2 + k : at + 3 + k] = part
    for x in range(layers):
        g_copies[x].wait()
        if 0 < x < layers - 1:
            phi_ref[x] = order_sum(lambda i: gbuf[i, x])
        to_north[x : x + 1] = phi_ref[x, rows - 1 : rows]
        to_south[x : x + 1] = phi_ref[x, 0:1]
    for s, x in enumerate(faces):
        for out, edge, inner, chosen in edges:
            at = layers + 3 + 6 * s
            out[at : at + 1] = gbuf[chosen[s], x, edge : edge + 1]
    for out in (to_north, to_south):
        out[layers + 14 : layers + 16] = jnp.zeros((2, out.shape[1]), f32)


def with_halo(ref, layer, below, above):
    rows = layer.shape[0]
    ref[8 : 8 + rows] = layer
    ref[7:8] = below
    ref[8 + rows : 9 + rows] = above


def corner_values(cells, planes, phi_ref, south_msg, north_msg, minus_wide, plus_wide):
    layers, rows, cols = phi_ref.shape
    cells[...] = jnp.ones_like(cells)
    for row in range(4):
        msg = south_msg if row < 2 else north_msg
        x = layers - 1 if row % 2 == 0 else 0
        beside = rows + (layers - 2 if row % 2 == 0 else 1)
        wide_row = 7 if row < 2 else rows + 8
        at = rows + layers
        first = at + 2 + 6 * (row % 2)
        far_phi = msg[at + row % 2 : at + row % 2 + 1]
        own_phi = phi_ref[x, 0:1] if row < 2 else phi_ref[x, rows - 1 : rows]
        parts = [msg[first + k : first + k + 1] for k in range(6)]
        parts.append(msg[rows + x : rows + x + 1])
        if row % 2 == 0:
            parts += [msg[beside : beside + 1], plus_wide[wide_row : wide_row + 1]]
        else:
            parts += [minus_wide[wide_row : wide_row + 1], msg[beside : beside + 1]]
        parts += [far_phi, own_phi] if row < 2 else [own_phi, far_phi]
        for k, part in enumerate(parts):
            cells[k, row : row + 1] = part
    place = lax.broadcasted_iota(jnp.int32, (8, cols), 0)
    is_top = (place == 0) | (place == 2)
    sx = jnp.where(is_top, 1.0, -1.0)
    sy = jnp.where(place < 2, 1.0, -1.0)
    delta = jnp.where(is_top, planes.up_jump, planes.low_jump)
    site = Site([cells[k] for k in range(2, 6)], *[cells[k] for k in range(6, 11)])
    w = lattice_weight[7]
    p = sx * site.u[0] + sy * site.u[1]
    q = sx * site.force[0] + sy * site.force[1]
    change = delta * (3.0 * sy + 9.0 * (sy * p) - 3.0 * site.u[1]) + 3.0 * (delta * delta)
    rp, gp = site.r * p, site.g_scale * p
    f_post = w * (site.k + p * (4.5 * rp + 3.375 * q) + 3.0 * rp + 1.125 * q + site.rho * change)
    g_post = w * (site.g_base + 4.5 * (gp * p) + 3.0 * gp + site.phi * change)
    return f_post - 0.25 * cells[0], g_post - (1.0 / 9.0) * cells[1]


def moment_kernel(
    sizes, after_north, after_south, offsets, f_ref, g_ref, faces, rims, rests
):
    layers, rows = f_ref.shape[1], f_ref.shape[2]
    count_x, count_y = sizes
    a = lax.axis_index("gx")
    for k, column in enumerate((lax.rem(a + 1, count_x), a)):
        is_plane, plane = plane_at(column, count_x)
        rest = jnp.clip(offsets[plane] - count_y // 2 * rows, 0, rows - 1)
        rest = jnp.where(is_plane, rest, 0).astype(f32)
        rests[k] = jnp.full(rests.shape[1:], rest, f32)
    for s, x in enumerate((layers - 1, 0)):
        for k, part in enumerate(moments_of(lambda i: f_ref[i, x])):
            faces[s, k] = part
    for s, (edge, chosen) in enumerate(((rows - 1, north_going), (0, south_going))):
        for k, part in enumerate(moments_of(lambda i: f_ref[i, :, edge, :])):
            rims[s, k] = part
        for j, i in enumerate(chosen):
            rims[s, 4 + j] = f_ref[i, :, edge, :]
            rims[s, 9 + j] = g_ref[i, :, edge, :]


def half_rows(rows, first):
    return slice(0, rows // 2) if first else slice(rows // 2, rows)


def seam_rows(rows, up):
    return slice(rows // 2 - 2, rows // 2) if up else slice(rows // 2, rows // 2 + 2)


def rim_values(rims, s, phi_ref, minus, plus, south_msg, north_msg, line, edge, chosen, out):
    layers, rows, cols = phi_ref.shape
    phi = phi_ref[:, edge, :]
    with_halo(line, phi, minus[edge : edge + 1], plus[edge : edge + 1])
    if edge == 0:
        below, above = south_msg[rows : rows + layers], phi_ref[:, 1, :]
    else:
        below, above = phi_ref[:, rows - 2, :], north_msg[rows : rows + layers]
    site = Site(
        [rims[s, k] for k in range(4)],
        phi,
        line[7 : 7 + layers],
        line[9 : 9 + layers],
        below,
        above,
    )
    for j, i in enumerate(chosen):
        cz = lattice_velocity[i][2]
        even, odd = site.pair_f(i)
        out[s, j] = z_moved(even + odd - 0.25 * rims[s, 4 + j], cz)
        even, odd = site.pair_g(i)
        out[s, 5 + j] = z_moved(even + odd - (1.0 / 9.0) * rims[s, 9 + j], cz)


def face_kernel(
    count_x,
    rests,
    f_ref,
    g_ref,
    face_moments,
    rims,
    phi_ref,
    rise,
    fall,
    south_msg,
    north_msg,
    mate,
    direct,
    direct_short,
    across,
    across_short,
    joint,
    cross,
    minus_out,
    plus_out,
    minus_wide,
    plus_wide,
    window,
    halo,
    line,
    rim_post,
    post,
    cells,
    corners,
    raw,
    wide,
):
    layers, rows, cols = phi_ref.shape
    planes = Planes([jnp.max(rests[k]).astype(jnp.int32) for k in range(2)], count_x)
    shear = Shear(raw, wide, rows)
    window[...] = jnp.zeros_like(window)
    for up in (True, False):
        if up:
            first, second = rise, north_msg
            near, far, start = planes.low_far, planes.low_near, planes.low_rest
        else:
            first, second = south_msg, fall
            near, far, start = planes.up_far, planes.up_near, rows - 1 - planes.up_rest
        target = minus_wide if up else plus_wide
        for k in range(window.shape[0]):
            lanes = slice(LANES * k, LANES * k + LANES)
            window[k, 8 : 8 + rows] = first[0:rows, lanes]
            window[k, 8 + rows : 8 + 2 * rows] = second[0:rows, lanes]
            target[:, lanes] = (
                near * window[k, pl.ds(start, rows + 16)]
                + far * window[k, pl.ds(start + 1, rows + 16)]
            )
    minus_out[...] = minus_wide[8 : 8 + rows]
    plus_out[...] = plus_wide[8 : 8 + rows]
    corners[0], corners[1] = corner_values(
        cells, planes, phi_ref, south_msg, north_msg, minus_wide, plus_wide
    )
    for s, (edge, chosen) in enumerate(((rows - 1, north_going), (0, south_going))):
        rim_values(
            rims,
            s,
            phi_ref,
            minus_out,
            plus_out,
            south_msg,
            north_msg,
            line,
            edge,
            chosen,
            rim_post,
        )
    for side, up in enumerate((True, False)):
        x = layers - 1 if up else 0
        delta = planes.up_jump if up else planes.low_jump
        with_halo(
            halo, phi_ref[x], south_msg[rows + x : rows + x + 1], north_msg[rows + x : rows + x + 1]
        )
        for h in range(0, rows, 8):
            span = slice(h, h + 8)
            phi_h = phi_ref[x, span]
            if up:
                minus, plus = phi_ref[x - 1, span], plus_wide[8 + h : 16 + h]
            else:
                minus, plus = minus_wide[8 + h : 16 + h], phi_ref[x + 1, span]
            site = Site(
                [face_moments[side, k, span] for k in range(4)],
                phi_h,
                minus,
                plus,
                halo[7 + h : 15 + h],
                halo[9 + h : 17 + h],
            )
            for j, i in enumerate(rising if up else falling):
                cz = lattice_velocity[i][2]
                change = lattice_weight[i] * site.jump(i, delta)
                even, odd = site.pair_f(i)
                value = even + odd - 0.25 * f_ref[i, x, span] + site.rho * change
                post[side, j, span] = z_moved(value, cz)
                even, odd = site.pair_g(i)
                value = even + odd - (1.0 / 9.0) * g_ref[i, x, span] + phi_h * change
                post[side, 5 + j, span] = z_moved(value, cz)

    part = rows // 2
    seam = 10 * part

    def hand_out(is_odd):
        for side, up in enumerate((True, False)):
            if up:
                near, far, rest = planes.up_near, planes.up_far, planes.up_rest
            else:
                near, far, rest = planes.low_near, planes.low_far, planes.low_rest
            first, second = (direct, mate) if up == is_odd else (joint, across)
            shear.clear()
            for j in range(10):
                cy = lattice_velocity[(rising if up else falling)[j % 5]][1]
                shear.put(post[side, j], up, near, far)
                corner = side + (0 if cy == 1 else 2)
                if cy == 1:
                    gate = jnp.where(rest == (0 if up else rows - 1), near, 0.0)
                    at = rows + 7 if up else rows + 8
                if cy == -1:
                    gate = jnp.where(rest == (rows - 1 if up else 0), far, 0.0)
                    at = 2 * rows + 7 if up else 2 * rows + 8
                if cy != 0:
                    shear.add_row(at, gate * corners[j // 5, corner : corner + 1])
                shear.take(up, 0, rest, cy, first, j)
                shear.take(up, 1, rest, cy, second, j)
        for j in range(10):
            mate[j, rows : rows + layers] = rim_post[1 if is_odd else 0, j]
            cross[j] = rim_post[0 if is_odd else 1, j]
            direct_short[j] = direct[j, half_rows(rows, is_odd)]
            across_short[part * j : part * j + part] = across[j, half_rows(rows, is_odd)]
            across_short[seam + 2 * j : seam + 2 * j + 2] = across[j, seam_rows(rows, not is_odd)]
        across_short[seam + 20 : seam + 24] = jnp.zeros((4, cols), f32)

    pl.when(planes.odd)(lambda: hand_out(True))
    pl.when(jnp.logical_not(planes.odd))(lambda: hand_out(False))


def bulk_kernel(
    after,
    f_ref,
    g_ref,
    phi_ref,
    minus,
    plus,
    south_msg,
    north_msg,
    mate_rim,
    cross_rim,
    next_f,
    next_g,
    wide_phi,
    halo,
):
    layers, rows, cols = phi_ref.shape
    is_odd = lax.rem(lax.axis_index("gy"), 2) == 1
    wide_phi[0] = minus[...]
    wide_phi[layers + 1] = plus[...]
    for x in range(layers):
        wide_phi[x + 1] = phi_ref[x]

    def layer(x, carry):
        with_halo(halo, phi_ref[x], south_msg[pl.ds(rows + x, 1)], north_msg[pl.ds(rows + x, 1)])
        beyond = lax.rem(x + 1, layers)
        before = lax.rem(x + layers - 1, layers)
        for h in range(0, rows, 8):
            span = slice(h, h + 8)
            phi_h = phi_ref[x, span]
            site = Site(
                moments_of(lambda i: f_ref[i, x, span]),
                phi_h,
                wide_phi[x, span],
                wide_phi[x + 2, span],
                halo[7 + h : 15 + h],
                halo[9 + h : 17 + h],
            )

            def emit(out, slot, i, value):
                cx, cy, cz = lattice_velocity[i]
                value = z_moved(value, cz)
                at = beyond if cx == 1 else before if cx == -1 else x
                if cy == 0:
                    out[i, at, span] = value
                elif cy == 1:
                    if h == 0:
                        rim = slot * 5 + north_going.index(i)
                        out[i, at, 0:1] = jnp.where(
                            is_odd, mate_rim[rim, pl.ds(rows + x, 1)], cross_rim[rim, pl.ds(x, 1)]
                        )
                    if h + 8 < rows:
                        out[i, at, h + 1 : h + 9] = value
                    else:
                        out[i, at, h + 1 : h + 8] = value[0:7]
                else:
                    if h + 8 == rows:
                        rim = slot * 5 + south_going.index(i)
                        out[i, at, rows - 1 : rows] = jnp.where(
                            is_odd, cross_rim[rim, pl.ds(x, 1)], mate_rim[rim, pl.ds(rows + x, 1)]
                        )
                    if h > 0:
                        out[i, at, h - 1 : h + 7] = value
                    else:
                        out[i, at, 0:7] = value[1:8]

            emit(next_f, 0, 0, lattice_weight[0] * site.k - 0.25 * f_ref[0, x, span])
            rest_g = (phi_h - 2.0 * site.mu - 0.5 * (phi_h * site.uu)) * (1.0 / 0.9)
            emit(next_g, 1, 0, rest_g - (1.0 / 9.0) * g_ref[0, x, span])
            for i in range(1, 19, 2):
                even, odd = site.pair_f(i)
                emit(next_f, 0, i, (even + odd) - 0.25 * f_ref[i, x, span])
                emit(next_f, 0, i + 1, (even - odd) - 0.25 * f_ref[i + 1, x, span])
                even, odd = site.pair_g(i)
                emit(next_g, 1, i, (even + odd) - (1.0 / 9.0) * g_ref[i, x, span])
                emit(next_g, 1, i + 1, (even - odd) - (1.0 / 9.0) * g_ref[i + 1, x, span])
        return carry

    lax.fori_loop(0, layers, layer, 0)


def put_faces(buf, out_f, out_g, chosen, x, sems):
    copies = [
        pltpu.make_async_copy(buf.at[5 * family + j], out.at[i, x], sems.at[5 * family + j])
        for family, out in enumerate((out_f, out_g))
        for j, i in enumerate(chosen)
    ]
    for copy in copies:
        copy.start()
    for copy in copies:
        copy.wait()


def merge_fill_kernel(
    count_x,
    long_planes,
    direct,
    direct_short,
    across,
    across_short,
    f_in,
    g_in,
    f_out,
    g_out,
    buf,
    sems,
):
    layers, rows = f_out.shape[1], f_out.shape[2]
    a = lax.axis_index("gx")
    odd = lax.rem(lax.axis_index("gy"), 2) == 1
    part = rows // 2
    seam = 10 * part

    def merge(column, up):
        near, other, between = half_rows(rows, up), half_rows(rows, not up), seam_rows(rows, up)
        chosen, x = (rising, 0) if up else (falling, layers - 1)
        copies = [
            pltpu.make_async_copy(
                buf.at[j], (f_out if j < 5 else g_out).at[chosen[j % 5], x], sems.at[j]
            )
            for j in range(10)
        ]

        def long():
            for j in range(10):
                buf[j, near] = across[j, near] + direct_short[j]
                buf[j, other] = across[j, other]
                copies[j].start()

        def short():
            for j in range(10):
                at = seam + 2 * j
                buf[j, near] = direct[j, near]
                buf[j, between] = direct[j, between] + across_short[at : at + 2]
                buf[j, other] = direct[j, other] + across_short[part * j : part * j + part]
                copies[j].start()

        is_plane, plane = plane_at(column, count_x)
        in_set = plane == long_planes[0]
        for k in long_planes[1:]:
            in_set = jnp.logical_or(in_set, plane == k)
        is_long = jnp.logical_and(is_plane, in_set)
        pl.when(is_long)(long)
        pl.when(jnp.logical_not(is_long))(short)
        for copy in copies:
            copy.wait()

    pl.when(odd)(lambda: merge(a, True))
    pl.when(jnp.logical_not(odd))(lambda: merge(lax.rem(a + 1, count_x), False))


def joint_fill_kernel(joint, f_in, g_in, f_out, g_out, sems):
    odd = lax.rem(lax.axis_index("gy"), 2) == 1
    layers = f_out.shape[1]
    pl.when(odd)(lambda: put_faces(joint, f_out, g_out, falling, layers - 1, sems))
    pl.when(jnp.logical_not(odd))(lambda: put_faces(joint, f_out, g_out, rising, 0, sems))


def on_device(momentum_dist, order_dist, offsets):
    layers, rows, cols = momentum_dist.shape[1:]
    count_x, count_y = lax.axis_size("gx"), lax.axis_size("gy")
    per_plane = count_x // 4
    half = count_y // 2

    def hop(value, target):
        perm = []
        for x in range(count_x):
            for y in range(count_y):
                tx, ty = target(x, y)
                perm.append((x * count_y + y, tx % count_x * count_y + ty % count_y))
        return lax.ppermute(value, ("gx", "gy"), perm)

    def base_up(x):
        return half if (x + 1) % per_plane == 0 else 0

    def base_low(x):
        return half if x % per_plane == 0 else 0

    def hop_parity(value, odd_up, extra):
        def target(x, y):
            if (y % 2 == 1) == odd_up:
                return (x + 1, y - base_up(x) - extra)
            return (x - 1, y + base_low(x) + extra)

        return hop(value, target)

    def hop_y(value, step):
        return hop(value, lambda x, y: (x, y + step))

    smem, vmem, anywhere = spec_of(pltpu.SMEM), spec_of(VMEM), spec_of(pl.ANY)
    plane = jax.ShapeDtypeStruct((rows, cols), f32)
    top, bottom = jnp.sum(order_dist[:, layers - 1], axis=0), jnp.sum(order_dist[:, 0], axis=0)
    rise = hop(top, lambda x, y: (x + 1, y - base_up(x)))
    fall = hop(bottom, lambda x, y: (x - 1, y + base_low(x)))

    block = jax.ShapeDtypeStruct((layers + 16, cols), f32)
    phi, to_north, to_south, order_near = pl.pallas_call(
        phi_kernel,
        out_shape=[jax.ShapeDtypeStruct((layers, rows, cols), f32)]
        + [block] * 2
        + [jax.ShapeDtypeStruct(order_dist.shape, f32)],
        in_specs=[anywhere, anywhere, vmem, vmem],
        out_specs=[vmem] * 4,
        scratch_shapes=[
            VMEM((19, 2, rows, cols), f32),
            pltpu.SemaphoreType.DMA((layers + 2,)),
        ],
        compiler_params=params(52 << 20),
        name="phi_all",
    )(momentum_dist, order_dist, top, bottom)
    to_north = jnp.concatenate([fall, to_north], 0)
    to_south = jnp.concatenate([rise, to_south], 0)
    south_msg, north_msg = hop_y(to_north, 1), hop_y(to_south, -1)

    face_moments, rims, rests = pl.pallas_call(
        functools.partial(moment_kernel, (count_x, count_y)),
        out_shape=[
            jax.ShapeDtypeStruct((2, 4, rows, cols), f32),
            jax.ShapeDtypeStruct((2, 14, layers, cols), f32),
            jax.ShapeDtypeStruct((2, 8, LANES), f32),
        ],
        in_specs=[anywhere, anywhere, smem, vmem, vmem],
        out_specs=[vmem] * 3,
        compiler_params=params(16 << 20),
        name="moments",
    )(to_north, to_south, offsets, momentum_dist, order_near)

    part = rows // 2
    ten = jax.ShapeDtypeStruct((10, rows, cols), f32)
    ten_short = jax.ShapeDtypeStruct((10, part, cols), f32)
    ten_seam = jax.ShapeDtypeStruct((10 * part + 24, cols), f32)
    side = jax.ShapeDtypeStruct((10, layers, cols), f32)
    ten_side = jax.ShapeDtypeStruct((10, rows + layers, cols), f32)
    *outgoing, minus, plus = pl.pallas_call(
        functools.partial(face_kernel, count_x),
        out_shape=[ten_side, ten, ten_short, ten, ten_seam, ten, side] + [plane] * 2,
        in_specs=[vmem] * 10,
        out_specs=[vmem] * 9,
        scratch_shapes=[
            VMEM((rows + 16, cols), f32),
            VMEM((rows + 16, cols), f32),
            VMEM((cols // LANES, 2 * rows + 16, LANES), f32),
            VMEM((rows + 16, cols), f32),
            VMEM((layers + 16, cols), f32),
            VMEM((2, 10, layers, cols), f32),
            VMEM((2, 10, rows, cols), f32),
            VMEM((11, 8, cols), f32),
            VMEM((2, 8, cols), f32),
            VMEM((cols // LANES, rows + 16, LANES), f32),
            VMEM((cols // LANES, 3 * rows + 16, LANES), f32),
        ],
        compiler_params=params(24 << 20),
        name="faces",
    )(
        rests,
        momentum_dist,
        order_near,
        face_moments,
        rims,
        phi,
        rise,
        fall,
        south_msg,
        north_msg,
    )
    around = (phi, minus, plus, south_msg, north_msg)
    whole = jax.ShapeDtypeStruct(momentum_dist.shape, f32)

    def finish(long_planes, mate, direct, direct_short, across, across_short, joint, cross):

        def is_long(x):
            return x % per_plane == 0 and x // per_plane % 4 in long_planes

        def hop_some(value, odd_up, extra, long):
            pairs = []
            for x in range(count_x):
                for y in range(count_y):
                    up = (y % 2 == 1) == odd_up
                    tx = (x + 1 if up else x - 1) % count_x
                    if is_long(tx if up else x) != long:
                        continue
                    ty = y - base_up(x) - extra if up else y + base_low(x) + extra
                    pairs.append((x * count_y + y, tx * count_y + ty % count_y))
            return lax.ppermute(value, ("gx", "gy"), pairs)

        cross = hop(cross, lambda x, y: (x, y + 1 if y % 2 == 1 else y - 1))
        mate = hop(mate, lambda x, y: (x, y ^ 1))
        direct, direct_short, across, across_short, cross = lax.optimization_barrier(
            (direct, direct_short, across, across_short, cross)
        )
        direct = hop_some(direct, True, 0, False)
        direct_short = hop_some(direct_short, True, 0, True)
        across = hop_some(across, False, 1, True)
        across_short = hop_some(across_short, False, 1, False)
        joint = joint + mate[:, :rows]
        after = joint
        joint = hop_parity(joint, False, 0)

        next_f, next_g = pl.pallas_call(
            bulk_kernel,
            out_shape=[whole, whole],
            in_specs=[anywhere] + [vmem] * 9,
            out_specs=[vmem] * 2,
            scratch_shapes=[
                VMEM((layers + 2, rows, cols), f32),
                VMEM((rows + 16, cols), f32),
            ],
            compiler_params=params(48 << 20),
            name="bulk",
        )(after, momentum_dist, order_near, *around, mate, cross)

        next_f, next_g = pl.pallas_call(
            joint_fill_kernel,
            out_shape=[whole, whole],
            in_specs=[vmem, anywhere, anywhere],
            out_specs=[anywhere, anywhere],
            scratch_shapes=[pltpu.SemaphoreType.DMA((10,))],
            input_output_aliases={1: 0, 2: 1},
            compiler_params=params(24 << 20),
            name="joint_fill",
        )(joint, next_f, next_g)

        return pl.pallas_call(
            functools.partial(merge_fill_kernel, count_x, sorted(long_planes)),
            out_shape=[whole, whole],
            in_specs=[vmem] * 4 + [anywhere, anywhere],
            out_specs=[anywhere, anywhere],
            scratch_shapes=[VMEM((10, rows, cols), f32), pltpu.SemaphoreType.DMA((10,))],
            input_output_aliases={4: 0, 5: 1},
            compiler_params=params(24 << 20),
            name="merge_fill",
        )(direct, direct_short, across, across_short, next_f, next_g)

    is_long = [(offsets[k] - half * rows > part).astype(jnp.int32) for k in (1, 2)]
    branches = [
        functools.partial(finish, {3} | ({1} if k & 2 else set()) | ({2} if k & 1 else set()))
        for k in range(4)
    ]
    return lax.switch(2 * is_long[0] + is_long[1], branches, *outgoing)


def solution(mesh):
    return jax.shard_map(
        on_device,
        mesh=mesh,
        in_specs=(P(None, "gx", "gy", None), P(None, "gx", "gy", None), P()),
        out_specs=(P(None, "gx", "gy", None), P(None, "gx", "gy", None)),
        check_vma=False,
    )
```

profile of v0, /device:TPU:0, one launch (start us, length us, event | category | flops | bytes accessed | tf_op | source)
XLA Modules:
  0.0 59.4 jit_solution(4380661591070071645)
XLA Ops:
  0.6 1.4 %slice_reduce_fusion = (f32[16,512]{1,0:T(8,128)S(1)}, f32[16,512]{1,0:T(8,128)S(1)}) fusion(f32[19,8,16,512]{3,2,1,0:T(8,128)} %g_ref.1), kind=kLoop, calls=%fused_computation.4 | loop fusion | flops 294912 | bytes 1310720 | tf_op jit(solution)/shard_map/reduce_sum | solution.py:661
  2.0 5.0 %collective-permute-start.29 = (f32[16,512]{1,0:T(8,128)S(1)}, f32[16,512]{1,0:T(8,128)S(1)}, u32[]{:S(2)}, u32[]{:S(2)}) collective-permute-start(f32[16,512]{1,0:T(8,128)S(1)} %get-tuple-element.248.top), channel_id=1, source_target_pairs={{0,12},{1,13},{2,14},{3,15},{4,8},{5,9},{6,10},{7,11},{8,20},{9,21... | collective-permute-start | bytes 98312 | tf_op jit(solution)/shard_map/ppermute | solution.py:640
  7.0 0.0 slice-start
  7.0 0.0 copy-start
  7.0 0.0 slice-start.1
  7.0 1.1 %collective-permute-start.28 = (f32[16,512]{1,0:T(8,128)S(1)}, f32[16,512]{1,0:T(8,128)S(1)}, u32[]{:S(2)}, u32[]{:S(2)}) collective-permute-start(f32[16,512]{1,0:T(8,128)S(1)} %get-tuple-element.249.bottom), channel_id=1, source_target_pairs={{0,28},{1,29},{2,30},{3,31},{4,24},{5,25},{6,26},{7,27},{8,4},{9,5... | collective-permute-start | bytes 98312 | tf_op jit(solution)/shard_map/ppermute | solution.py:640
  8.1 3.3 %phi_all.1 = (f32[8,16,512]{2,1,0:T(8,128)S(1)}, f32[24,512]{1,0:T(8,128)S(1)}, f32[24,512]{1,0:T(8,128)S(1)}, f32[19,8,16,512]{3,2,1,0:T(8,128)S(1)}) custom-call(f32[19,8,16,512]{3,2,1,0:T(8,128)} %f_ref.5, f32[19,8,16,512]{3,2,1,0:T(8,128)} %g_ref.1, f32[16,512]{1,0:T(8,128)S(1)} %get-tuple-element.248.top, f32[16,512]{1,0:T(8,128)S(1)} %get-tuple-element.249.bottom), custom_call_target="tpu_custom_call" | custom-call | tf_op jit(solution)/shard_map/phi_all/pallas_call | solution.py:666
  11.4 0.0 collective-permute-done.29.rise
  11.4 2.2 %collective-permute-start.31 = (f32[40,512]{1,0:T(8,128)S(1)}, f32[40,512]{1,0:T(8,128)S(1)}, u32[]{:S(2)}, u32[]{:S(2)}) collective-permute-start(f32[40,512]{1,0:T(8,128)S(1)} %constant_dynamic-update-slice_fusion.2.after_south), channel_id=1, source_target_pairs={{0,7},{1,0},{2,1},{3,2},{4,3},{5,4},{6,5},{7,6},{8,15},{9,8},{10,9... | collective-permute-start | bytes 245768 | tf_op jit(solution)/shard_map/ppermute | solution.py:640
  13.7 0.0 collective-permute-done.28.fall
  13.7 0.1 collective-permute-start.30
  13.7 0.0 copy-done
  13.8 0.6 fusion
  15.6 0.0 slice-done
  15.7 0.0 slice-done.1
  15.7 1.0 %moments.1 = (f32[2,4,16,512]{3,2,1,0:T(8,128)S(1)}, f32[2,14,8,512]{3,2,1,0:T(8,128)S(1)}, f32[2,8,128]{2,1,0:T(8,128)S(1)}) custom-call(f32[40,512]{1,0:T(8,128)S(1)} %constant_dynamic-update-slice_fusion.after_north, f32[40,512]{1,0:T(8,128)S(1)} %constant_dynamic-update-slice_fusion.2.after_south, s32[4]{0:T(128)S(1)} %copy-done, ...), custom_call_target="tpu_custom_call" | custom-call | tf_op jit(solution)/shard_map/moments/pallas_call | solution.py:684
  16.6 0.0 collective-permute-done.31.north_msg
  16.7 2.7 %collective-permute-done.30.south_msg = f32[40,512]{1,0:T(8,128)S(1)} collective-permute-done((f32[40,512]{1,0:T(8,128)S(1)}, f32[40,512]{1,0:T(8,128)S(1)}, u32[]{:S(2)}, u32[]{:S(2)}) %collective-permute-start.30) | collective-permute-done | bytes 81952 | tf_op jit(solution)/shard_map/ppermute | solution.py:640
  19.4 1.5 %faces.1 = (f32[10,24,512]{2,1,0:T(8,128)S(1)}, f32[10,16,512]{2,1,0:T(8,128)S(1)}, f32[10,8,512]{2,1,0:T(8,128)S(1)}, f32[10,16,512]{2,1,0:T(8,128)S(1)}, f32[1...) custom-call(f32[2,8,128]{2,1,0:T(8,128)S(1)} %get-tuple-element.225., ...), custom_call_target="tpu_custom_call" | custom-call | tf_op jit(solution)/shard_map/faces/pallas_call | solution.py:703
  20.9 38.4 %conditional.1 = ((f32[19,8,16,512]{3,2,1,0:T(8,128)}, f32[19,8,16,512]{3,2,1,0:T(8,128)})) conditional(s32[]{:T(128)} %bitcast, (f32[10,8,512]{2,1,0:T(8,128)S(1)}, f32[10,16,512]{2,1,0:T(8,128)S(1)}, f32[10,8,512]{2,1,0:T(8,128)S(1)}, f32[10,16,512]{2,1,0:T(8,128)S(1)}, f32[104,512]{1,0:T(8,128)S(1)}, ...), branch_computations={%region_2.0_spmd, %region_3.0_spmd, %region_4.0_spmd, %region_5.0_... | conditional | flops 81920 | bytes 9044256 | solution.py:808
  21.0 0.1 collective-permute-start.12
  21.1 0.9 %collective-permute-start.7 = (f32[10,8,512]{2,1,0:T(8,128)S(1)}, f32[10,8,512]{2,1,0:T(8,128)S(1)}, u32[]{:S(2)}, u32[]{:S(2)}) collective-permute-start(f32[10,8,512]{2,1,0:T(8,128)S(1)} %get-tuple-element.139), channel_id=1, source_target_pairs={{0,7},{1,2},{2,1},{3,4},{4,3},{5,6},{6,5},{7,0},{8,15},{9,10},{10,... | collective-permute-start | bytes 491528 | tf_op jit(solution)/shard_map/cond/branch_1_fun/ppermute | solution.py:640
  21.9 1.0 %collective-permute-done.12.mate_rim = f32[10,24,512]{2,1,0:T(8,128)S(1)} collective-permute-done((f32[10,24,512]{2,1,0:T(8,128)S(1)}, f32[10,24,512]{2,1,0:T(8,128)S(1)}, u32[]{:S(2)}, u32[]{:S(2)}) %collective-permute-start.12) | collective-permute-done | bytes 491552 | tf_op jit(solution)/shard_map/cond/branch_1_fun/ppermute | solution.py:640
  23.0 0.4 collective-permute-start.13
  23.4 4.4 %collective-permute-done.7.cross_rim = f32[10,8,512]{2,1,0:T(8,128)S(1)} collective-permute-done((f32[10,8,512]{2,1,0:T(8,128)S(1)}, f32[10,8,512]{2,1,0:T(8,128)S(1)}, u32[]{:S(2)}, u32[]{:S(2)}) %collective-permute-start.7) | collective-permute-done | bytes 163872 | tf_op jit(solution)/shard_map/cond/branch_1_fun/ppermute | solution.py:640
  27.8 0.7 %collective-permute-start.10 = (f32[10,16,512]{2,1,0:T(8,128)S(1)}, f32[10,16,512]{2,1,0:T(8,128)S(1)}, u32[]{:S(2)}, u32[]{:S(2)}) collective-permute-start(f32[10,16,512]{2,1,0:T(8,128)S(1)} %get-tuple-element.142), channel_id=1, source_target_pairs={{8,19},{10,21},{12,23},{14,17},{16,27},{17,14},{18,29},{19,8},{20,... | collective-permute-start | bytes 983048 | tf_op jit(solution)/shard_map/cond/branch_1_fun/ppermute | solution.py:753
  28.4 1.9 %collective-permute-start.8 = (f32[10,16,512]{2,1,0:T(8,128)S(1)}, f32[10,16,512]{2,1,0:T(8,128)S(1)}, u32[]{:S(2)}, u32[]{:S(2)}) collective-permute-start(f32[10,16,512]{2,1,0:T(8,128)S(1)} %get-tuple-element.140), channel_id=1, source_target_pairs={{0,28},{1,13},{2,30},{3,15},{4,24},{5,9},{6,26},{7,11},{8,4},{10,6... | collective-permute-start | bytes 983048 | tf_op jit(solution)/shard_map/cond/branch_1_fun/ppermute | solution.py:753
  30.4 1.9 %collective-permute-start.11 = (f32[104,512]{1,0:T(8,128)S(1)}, f32[104,512]{1,0:T(8,128)S(1)}, u32[]{:S(2)}, u32[]{:S(2)}) collective-permute-start(f32[104,512]{1,0:T(8,128)S(1)} %get-tuple-element.143), channel_id=1, source_target_pairs={{0,11},{1,30},{2,13},{3,24},{4,15},{5,26},{6,9},{7,28},{9,6},{11,0... | collective-permute-start | bytes 638984 | tf_op jit(solution)/shard_map/cond/branch_1_fun/ppermute | solution.py:753
  32.3 0.7 %collective-permute-start.9 = (f32[10,8,512]{2,1,0:T(8,128)S(1)}, f32[10,8,512]{2,1,0:T(8,128)S(1)}, u32[]{:S(2)}, u32[]{:S(2)}) collective-permute-start(f32[10,8,512]{2,1,0:T(8,128)S(1)} %get-tuple-element.141), channel_id=1, source_target_pairs={{9,21},{11,23},{13,17},{15,19},{16,12},{17,29},{18,14},{19,31},{20... | collective-permute-start | bytes 491528 | tf_op jit(solution)/shard_map/cond/branch_1_fun/ppermute | solution.py:753
  33.0 9.0 %bulk.5 = (f32[19,8,16,512]{3,2,1,0:T(8,128)}, f32[19,8,16,512]{3,2,1,0:T(8,128)}) custom-call(f32[10,16,512]{2,1,0:T(8,128)S(1)} %slice_add_fusion.1.after, f32[19,8,16,512]{3,2,1,0:T(8,128)S(1)} %get-tuple-element.146.f_ref, f32[19,8,16,512]{3,2,1,0:T(8,128)S(1)} %get-tuple-element.147.g_ref, f32[8,16,512]{2,1,0:T(8,128)S(1)} %get-tuple-element.148.phi_ref, ...), custom_call_target="tpu_custom_call" | custom-call | tf_op jit(solution)/shard_map/cond/branch_1_fun/bulk/pallas_call | solution.py:768
  42.0 8.4 %collective-permute-done.13.joint = f32[10,16,512]{2,1,0:T(8,128)S(1)} collective-permute-done((f32[10,16,512]{2,1,0:T(8,128)S(1)}, f32[10,16,512]{2,1,0:T(8,128)S(1)}, u32[]{:S(2)}, u32[]{:S(2)}) %collective-permute-start.13) | collective-permute-done | bytes 327712 | tf_op jit(solution)/shard_map/cond/branch_1_fun/ppermute | solution.py:640
  50.4 0.8 %joint_fill.5 = (f32[19,8,16,512]{3,2,1,0:T(8,128)}, f32[19,8,16,512]{3,2,1,0:T(8,128)}) custom-call(f32[10,16,512]{2,1,0:T(8,128)S(1)} %collective-permute-done.13.joint, f32[19,8,16,512]{3,2,1,0:T(8,128)} %get-tuple-element.154.f_in, f32[19,8,16,512]{3,2,1,0:T(8,128)} %get-tuple-element.155.g_in), custom_call_target="tpu_custom_call", output_to_operand_aliasing={{0}: (1, {}), {1}: (2, {})} | custom-call | tf_op jit(solution)/shard_map/cond/branch_1_fun/joint_fill/pallas_call | solution.py:781
  51.2 0.0 collective-permute-done.9.direct_short
  51.2 0.0 collective-permute-done.11.across_short
  51.2 0.0 collective-permute-done.10.across
  51.2 7.4 %collective-permute-done.8.direct = f32[10,16,512]{2,1,0:T(8,128)S(1)} collective-permute-done((f32[10,16,512]{2,1,0:T(8,128)S(1)}, f32[10,16,512]{2,1,0:T(8,128)S(1)}, u32[]{:S(2)}, u32[]{:S(2)}) %collective-permute-start.8) | collective-permute-done | bytes 327712 | tf_op jit(solution)/shard_map/cond/branch_1_fun/ppermute | solution.py:753
  58.6 0.8 %merge_fill.5 = (f32[19,8,16,512]{3,2,1,0:T(8,128)}, f32[19,8,16,512]{3,2,1,0:T(8,128)}) custom-call(f32[10,16,512]{2,1,0:T(8,128)S(1)} %collective-permute-done.8.direct, f32[10,8,512]{2,1,0:T(8,128)S(1)} %collective-permute-done.9.direct_short, f32[10,16,512]{2,1,0:T(8,128)S(1)} %collective-permute-done.10.across, ...), custom_call_target="tpu_custom_call", output_to_operand_aliasing={{0}: (4, {}), {1}: (5, {})} | custom-call | tf_op jit(solution)/shard_map/cond/branch_1_fun/merge_fill/pallas_call | solution.py:792
  (6 shorter events, 0.1 us)
Async XLA Ops:
  2.0 9.4 %collective-permute-start.29 = (f32[16,512]{1,0:T(8,128)S(1)}, f32[16,512]{1,0:T(8,128)S(1)}, u32[]{:S(2)}, u32[]{:S(2)}) collective-permute-start(f32[16,512]{1,0:T(8,128)S(1)} %get-tuple-element.248.top), channel_id=1, source_target_pairs={{0,12},{1,13},{2,14},{3,15},{4,8},{5,9},{6,10},{7,11},{8,20},{9,21... | collective-permute-start | bytes 98312 | tf_op jit(solution)/shard_map/ppermute | solution.py:640
  7.0 8.6 %slice-start = ((s8[4980736]{0:T(1024)(128)(4,1)}), s8[4194304]{0:T(1024)(128)(4,1)S(1)}, s32[]{:S(2)}) async-start(s8[4980736]{0:T(1024)(128)(4,1)} %bitcast.1), calls=%async_computation | async-start | bytes 8388608
  7.0 6.7 %copy-start = (s32[4]{0:T(128)S(1)}, s32[4]{0:T(128)}, u32[]{:S(2)}) copy-start(s32[4]{0:T(128)} %offsets.1) | copy-start | bytes 52
  7.0 8.7 %slice-start.1 = ((s8[4980736]{0:T(1024)(128)(4,1)}), s8[786432]{0:T(1024)(128)(4,1)S(1)}, s32[]{:S(2)}) async-start(s8[4980736]{0:T(1024)(128)(4,1)} %bitcast.1), calls=%async_computation.1 | async-start | bytes 1572864
  7.0 6.7 %collective-permute-start.28 = (f32[16,512]{1,0:T(8,128)S(1)}, f32[16,512]{1,0:T(8,128)S(1)}, u32[]{:S(2)}, u32[]{:S(2)}) collective-permute-start(f32[16,512]{1,0:T(8,128)S(1)} %get-tuple-element.249.bottom), channel_id=1, source_target_pairs={{0,28},{1,29},{2,30},{3,31},{4,24},{5,25},{6,26},{7,27},{8,4},{9,5... | collective-permute-start | bytes 98312 | tf_op jit(solution)/shard_map/ppermute | solution.py:640
  11.4 5.2 %collective-permute-start.31 = (f32[40,512]{1,0:T(8,128)S(1)}, f32[40,512]{1,0:T(8,128)S(1)}, u32[]{:S(2)}, u32[]{:S(2)}) collective-permute-start(f32[40,512]{1,0:T(8,128)S(1)} %constant_dynamic-update-slice_fusion.2.after_south), channel_id=1, source_target_pairs={{0,7},{1,0},{2,1},{3,2},{4,3},{5,4},{6,5},{7,6},{8,15},{9,8},{10,9... | collective-permute-start | bytes 245768 | tf_op jit(solution)/shard_map/ppermute | solution.py:640
  13.7 5.7 %collective-permute-start.30 = (f32[40,512]{1,0:T(8,128)S(1)}, f32[40,512]{1,0:T(8,128)S(1)}, u32[]{:S(2)}, u32[]{:S(2)}) collective-permute-start(f32[40,512]{1,0:T(8,128)S(1)} %constant_dynamic-update-slice_fusion.after_north), channel_id=1, source_target_pairs={{0,1},{1,2},{2,3},{3,4},{4,5},{5,6},{6,7},{7,0},{8,9},{9,10},{10,1... | collective-permute-start | bytes 245768 | tf_op jit(solution)/shard_map/ppermute | solution.py:640
  21.0 1.9 %collective-permute-start.12 = (f32[10,24,512]{2,1,0:T(8,128)S(1)}, f32[10,24,512]{2,1,0:T(8,128)S(1)}, u32[]{:S(2)}, u32[]{:S(2)}) collective-permute-start(f32[10,24,512]{2,1,0:T(8,128)S(1)} %get-tuple-element.145), channel_id=1, source_target_pairs={{0,1},{1,0},{2,3},{3,2},{4,5},{5,4},{6,7},{7,6},{8,9},{9,8},{10,11... | collective-permute-start | bytes 1474568 | tf_op jit(solution)/shard_map/cond/branch_1_fun/ppermute | solution.py:640
  21.1 6.7 %collective-permute-start.7 = (f32[10,8,512]{2,1,0:T(8,128)S(1)}, f32[10,8,512]{2,1,0:T(8,128)S(1)}, u32[]{:S(2)}, u32[]{:S(2)}) collective-permute-start(f32[10,8,512]{2,1,0:T(8,128)S(1)} %get-tuple-element.139), channel_id=1, source_target_pairs={{0,7},{1,2},{2,1},{3,4},{4,3},{5,6},{6,5},{7,0},{8,15},{9,10},{10,... | collective-permute-start | bytes 491528 | tf_op jit(solution)/shard_map/cond/branch_1_fun/ppermute | solution.py:640
  23.0 27.4 %collective-permute-start.13 = (f32[10,16,512]{2,1,0:T(8,128)S(1)}, f32[10,16,512]{2,1,0:T(8,128)S(1)}, u32[]{:S(2)}, u32[]{:S(2)}) collective-permute-start(f32[10,16,512]{2,1,0:T(8,128)S(1)} %slice_add_fusion.1.after), channel_id=1, source_target_pairs={{0,12},{1,29},{2,14},{3,31},{4,8},{5,25},{6,10},{7,27},{8,20},{9,5... | collective-permute-start | bytes 983048 | tf_op jit(solution)/shard_map/cond/branch_1_fun/ppermute | solution.py:640
  27.8 23.4 %collective-permute-start.10 = (f32[10,16,512]{2,1,0:T(8,128)S(1)}, f32[10,16,512]{2,1,0:T(8,128)S(1)}, u32[]{:S(2)}, u32[]{:S(2)}) collective-permute-start(f32[10,16,512]{2,1,0:T(8,128)S(1)} %get-tuple-element.142), channel_id=1, source_target_pairs={{8,19},{10,21},{12,23},{14,17},{16,27},{17,14},{18,29},{19,8},{20,... | collective-permute-start | bytes 983048 | tf_op jit(solution)/shard_map/cond/branch_1_fun/ppermute | solution.py:753
  28.4 30.1 %collective-permute-start.8 = (f32[10,16,512]{2,1,0:T(8,128)S(1)}, f32[10,16,512]{2,1,0:T(8,128)S(1)}, u32[]{:S(2)}, u32[]{:S(2)}) collective-permute-start(f32[10,16,512]{2,1,0:T(8,128)S(1)} %get-tuple-element.140), channel_id=1, source_target_pairs={{0,28},{1,13},{2,30},{3,15},{4,24},{5,9},{6,26},{7,11},{8,4},{10,6... | collective-permute-start | bytes 983048 | tf_op jit(solution)/shard_map/cond/branch_1_fun/ppermute | solution.py:753
  30.4 20.8 %collective-permute-start.11 = (f32[104,512]{1,0:T(8,128)S(1)}, f32[104,512]{1,0:T(8,128)S(1)}, u32[]{:S(2)}, u32[]{:S(2)}) collective-permute-start(f32[104,512]{1,0:T(8,128)S(1)} %get-tuple-element.143), channel_id=1, source_target_pairs={{0,11},{1,30},{2,13},{3,24},{4,15},{5,26},{6,9},{7,28},{9,6},{11,0... | collective-permute-start | bytes 638984 | tf_op jit(solution)/shard_map/cond/branch_1_fun/ppermute | solution.py:753
  32.3 18.9 %collective-permute-start.9 = (f32[10,8,512]{2,1,0:T(8,128)S(1)}, f32[10,8,512]{2,1,0:T(8,128)S(1)}, u32[]{:S(2)}, u32[]{:S(2)}) collective-permute-start(f32[10,8,512]{2,1,0:T(8,128)S(1)} %get-tuple-element.141), channel_id=1, source_target_pairs={{9,21},{11,23},{13,17},{15,19},{16,12},{17,29},{18,14},{19,31},{20... | collective-permute-start | bytes 491528 | tf_op jit(solution)/shard_map/cond/branch_1_fun/ppermute | solution.py:753
where the time goes:
time: 59.9 us; the launch traced here: 59.4 us
  waiting for transfers between devices  23.9 us (40%)
  Pallas kernels  16.4 us (27%)
  starting transfers between devices  14.9 us (25%)
  between operations  2.04 us (3%)
  other arithmetic  1.41 us (2%)
  local copies, waits for them, and re-layouts  0.62 us (1%)
    ppermute x7, waiting for transfers between devices, hop(): return lax.ppermute(value, ('gx', 'gy'), perm)  16.5 us
    ppermute x7, starting transfers between devices, hop(): return lax.ppermute(value, ('gx', 'gy'), perm)  9.75 us
    pallas_call x1, Pallas kernels, finish(): pl.pallas_call(bulk_kernel, out_shape=[whole, whole], in_specs=[anywhere]...  9 us
    ppermute x4, waiting for transfers between devices, hop_some(): return lax.ppermute(value, ('gx', 'gy'), pairs)  7.36 us
    ppermute x4, starting transfers between devices, hop_some(): return lax.ppermute(value, ('gx', 'gy'), pairs)  5.18 us
    pallas_call x1, Pallas kernels, on_device(): pl.pallas_call(phi_kernel, out_shape=[jax.ShapeDtypeStruct((layers, rows,...  3.31 us
    pallas_call x1, Pallas kernels, on_device(): pl.pallas_call(functools.partial(face_kernel, count_x), out_shape=[ten_si...  1.55 us
    reduce_sum x1, other arithmetic, on_device(): jnp.sum(order_dist[:, layers - 1], axis=0)  1.36 us
  transfers between devices with their start and end apart: 11, of which 5 were waited for; matrix products, arithmetic and copies ran while one was open for 1% of the time, Pallas kernels for 24%

commit v1 on v0

--- a/solution.py
+++ b/solution.py
@@ -192,39 +192,38 @@
     return total
 
 
-def phi_kernel(f_ref, g_ref, top, bottom, phi_ref, to_north, to_south, gbuf, fbuf, sems):
+def gate_kernel(g_ref, out):
+    out[...] = jnp.zeros_like(out)
+
+
+def phi_kernel(gate, f_ref, g_ref, top, bottom, phi_ref, to_north, to_south, fbuf, sems):
     layers, rows = phi_ref.shape[0], phi_ref.shape[1]
     faces = (layers - 1, 0)
-    f_copies = [
-        pltpu.make_async_copy(f_ref.at[:, x], fbuf.at[:, s], sems.at[layers + s])
+    copies = [
+        pltpu.make_async_copy(f_ref.at[:, x], fbuf.at[:, s], sems.at[s])
         for s, x in enumerate(faces)
     ]
-    g_copies = [
-        pltpu.make_async_copy(g_ref.at[:, x], gbuf.at[:, x], sems.at[x]) for x in range(layers)
-    ]
-    for copy in f_copies + g_copies:
+    for copy in copies:
         copy.start()
     phi_ref[layers - 1] = top[...]
     phi_ref[0] = bottom[...]
-    edges = ((to_north, rows - 1, rows - 2, (7, 10)), (to_south, 0, 1, (9, 8)))
+    for x in range(layers):
+        if 0 < x < layers - 1:
+            phi_ref[x] = order_sum(lambda i: g_ref[i, x])
+        to_north[x : x + 1] = phi_ref[x, rows - 1 : rows]
+        to_south[x : x + 1] = phi_ref[x, 0:1]
     for s, x in enumerate(faces):
-        f_copies[s].wait()
-        for out, edge, inner, chosen in edges:
+        copies[s].wait()
+        for out, edge, inner, chosen in (
+            (to_north, rows - 1, rows - 2, (7, 10)),
+            (to_south, 0, 1, (9, 8)),
+        ):
             out[layers + s : layers + s + 1] = phi_ref[x, inner : inner + 1]
             at = layers + 2 + 6 * s
             out[at : at + 1] = fbuf[chosen[s], s, edge : edge + 1]
+            out[at + 1 : at + 2] = g_ref[chosen[s], x, edge : edge + 1]
             for k, part in enumerate(moments_of(lambda i: fbuf[i, s, edge : edge + 1])):
                 out[at + 2 + k : at + 3 + k] = part
-    for x in range(layers):
-        g_copies[x].wait()
-        if 0 < x < layers - 1:
-            phi_ref[x] = order_sum(lambda i: gbuf[i, x])
-        to_north[x : x + 1] = phi_ref[x, rows - 1 : rows]
-        to_south[x : x + 1] = phi_ref[x, 0:1]
-    for s, x in enumerate(faces):
-        for out, edge, inner, chosen in edges:
-            at = layers + 3 + 6 * s
-            out[at : at + 1] = gbuf[chosen[s], x, edge : edge + 1]
     for out in (to_north, to_south):
         out[layers + 14 : layers + 16] = jnp.zeros((2, out.shape[1]), f32)
 
@@ -663,20 +662,23 @@
     fall = hop(bottom, lambda x, y: (x - 1, y + base_low(x)))
 
     block = jax.ShapeDtypeStruct((layers + 16, cols), f32)
-    phi, to_north, to_south, order_near = pl.pallas_call(
+    gate = pl.pallas_call(
+        gate_kernel,
+        out_shape=jax.ShapeDtypeStruct((8, LANES), f32),
+        in_specs=[anywhere],
+        out_specs=vmem,
+        compiler_params=params(50 << 20),
+        name="gate",
+    )(order_dist)
+    phi, to_north, to_south = pl.pallas_call(
         phi_kernel,
-        out_shape=[jax.ShapeDtypeStruct((layers, rows, cols), f32)]
-        + [block] * 2
-        + [jax.ShapeDtypeStruct(order_dist.shape, f32)],
-        in_specs=[anywhere, anywhere, vmem, vmem],
-        out_specs=[vmem] * 4,
-        scratch_shapes=[
-            VMEM((19, 2, rows, cols), f32),
-            pltpu.SemaphoreType.DMA((layers + 2,)),
-        ],
-        compiler_params=params(52 << 20),
+        out_shape=[jax.ShapeDtypeStruct((layers, rows, cols), f32)] + [block] * 2,
+        in_specs=[anywhere, anywhere, vmem, vmem, vmem],
+        out_specs=[vmem] * 3,
+        scratch_shapes=[VMEM((19, 2, rows, cols), f32), pltpu.SemaphoreType.DMA((2,))],
+        compiler_params=params(8 << 20),
         name="phi_all",
-    )(momentum_dist, order_dist, top, bottom)
+    )(gate, momentum_dist, order_dist, top, bottom)
     to_north = jnp.concatenate([fall, to_north], 0)
     to_south = jnp.concatenate([rise, to_south], 0)
     south_msg, north_msg = hop_y(to_north, 1), hop_y(to_south, -1)
@@ -692,7 +694,7 @@
         out_specs=[vmem] * 3,
         compiler_params=params(16 << 20),
         name="moments",
-    )(to_north, to_south, offsets, momentum_dist, order_near)
+    )(to_north, to_south, offsets, momentum_dist, order_dist)
 
     part = rows // 2
     ten = jax.ShapeDtypeStruct((10, rows, cols), f32)
@@ -723,7 +725,7 @@
     )(
         rests,
         momentum_dist,
-        order_near,
+        order_dist,
         face_moments,
         rims,
         phi,
@@ -776,7 +778,7 @@
             ],
             compiler_params=params(48 << 20),
             name="bulk",
-        )(after, momentum_dist, order_near, *around, mate, cross)
+        )(after, momentum_dist, order_dist, *around, mate, cross)
 
         next_f, next_g = pl.pallas_call(
             joint_fill_kernel,

time: 59.9 us -> 57.2 us (0.955)
  the two profiles are of different devices: /device:TPU:0 before, /device:TPU:3 now
where the time goes in v1:
time: 57.2 us; the launch traced here: 56.6 us
  starting transfers between devices  19.1 us (33%)
  waiting for transfers between devices  18.7 us (33%)
  Pallas kernels  14.5 us (25%)
  between operations  2.05 us (4%)
  other arithmetic  1.55 us (3%)
  local copies, waits for them, and re-layouts  0.63 us (1%)
    ppermute x7, waiting for transfers between devices, hop(): return lax.ppermute(value, ('gx', 'gy'), perm)  11.5 us
    ppermute x7, starting transfers between devices, hop(): return lax.ppermute(value, ('gx', 'gy'), perm)  10.2 us
    ppermute x4, starting transfers between devices, hop_some(): return lax.ppermute(value, ('gx', 'gy'), pairs)  8.93 us
    pallas_call x1, Pallas kernels, finish(): pl.pallas_call(bulk_kernel, out_shape=[whole, whole], in_specs=[anywhere]...  8.9 us
    ppermute x4, waiting for transfers between devices, hop_some(): return lax.ppermute(value, ('gx', 'gy'), pairs)  7.21 us
    pallas_call x1, Pallas kernels, on_device(): pl.pallas_call(functools.partial(face_kernel, count_x), out_shape=[ten_si...  1.55 us
    reduce_sum x1, other arithmetic, on_device(): jnp.sum(order_dist[:, layers - 1], axis=0)  1.51 us
    pallas_call x1, Pallas kernels, on_device(): pl.pallas_call(phi_kernel, out_shape=[jax.ShapeDtypeStruct((layers, rows,...  1.47 us
  transfers between devices with their start and end apart: 11, of which 5 were waited for; matrix products, arithmetic and copies ran while one was open for 1% of the time, Pallas kernels for 21%

profile of v1, /device:TPU:3, one launch (start us, length us, event | category | flops | bytes accessed | tf_op | source)
XLA Modules:
  0.0 56.6 jit_solution(1472605238060473672)
XLA Ops:
  0.6 0.0 copy-start.1
  0.6 1.5 %slice_reduce_fusion = (f32[16,512]{1,0:T(8,128)S(1)}, f32[16,512]{1,0:T(8,128)S(1)}) fusion(f32[19,8,16,512]{3,2,1,0:T(8,128)} %g_ref.7), kind=kLoop, calls=%fused_computation.4 | loop fusion | flops 294912 | bytes 1310720 | tf_op jit(solution)/shard_map/reduce_sum | solution.py:660
  2.2 3.3 %collective-permute-start.29 = (f32[16,512]{1,0:T(8,128)S(1)}, f32[16,512]{1,0:T(8,128)S(1)}, u32[]{:S(2)}, u32[]{:S(2)}) collective-permute-start(f32[16,512]{1,0:T(8,128)S(1)} %get-tuple-element.246.top), channel_id=1, source_target_pairs={{0,12},{1,13},{2,14},{3,15},{4,8},{5,9},{6,10},{7,11},{8,20},{9,21... | collective-permute-start | bytes 98312 | tf_op jit(solution)/shard_map/ppermute | solution.py:639
  5.4 0.0 collective-permute-start.28
  5.5 0.0 slice-start
  5.5 0.0 copy-done.1
  5.5 0.0 copy-start
  5.5 0.0 slice-start.1
  5.5 1.5 %phi_all.1 = (f32[8,16,512]{2,1,0:T(8,128)S(1)}, f32[24,512]{1,0:T(8,128)S(1)}, f32[24,512]{1,0:T(8,128)S(1)}) custom-call(f32[8,128]{1,0:T(8,128)S(1)} %gate.1, f32[19,8,16,512]{3,2,1,0:T(8,128)} %f_ref.5, f32[19,8,16,512]{3,2,1,0:T(8,128)S(1)} %copy-done.1, f32[16,512]{1,0:T(8,128)S(1)} %get-tuple-element.246.top, f32[16,512]{1,0:T(8,128)S(1)} %get-tuple-element.247.bottom), custom_call_target="tpu_custom_call" | custom-call | tf_op jit(solution)/shard_map/phi_all/pallas_call | solution.py:673
  7.0 0.0 collective-permute-done.29.rise
  7.0 1.9 %collective-permute-start.31 = (f32[40,512]{1,0:T(8,128)S(1)}, f32[40,512]{1,0:T(8,128)S(1)}, u32[]{:S(2)}, u32[]{:S(2)}) collective-permute-start(f32[40,512]{1,0:T(8,128)S(1)} %constant_dynamic-update-slice_fusion.2.after_south), channel_id=1, source_target_pairs={{0,7},{1,0},{2,1},{3,2},{4,3},{5,4},{6,5},{7,6},{8,15},{9,8},{10,9... | collective-permute-start | bytes 245768 | tf_op jit(solution)/shard_map/ppermute | solution.py:639
  8.9 2.0 %collective-permute-done.28.fall = f32[16,512]{1,0:T(8,128)S(1)} collective-permute-done((f32[16,512]{1,0:T(8,128)S(1)}, f32[16,512]{1,0:T(8,128)S(1)}, u32[]{:S(2)}, u32[]{:S(2)}) %collective-permute-start.28) | collective-permute-done | bytes 32800 | tf_op jit(solution)/shard_map/ppermute | solution.py:639
  10.9 3.3 %collective-permute-start.30 = (f32[40,512]{1,0:T(8,128)S(1)}, f32[40,512]{1,0:T(8,128)S(1)}, u32[]{:S(2)}, u32[]{:S(2)}) collective-permute-start(f32[40,512]{1,0:T(8,128)S(1)} %constant_dynamic-update-slice_fusion.after_north), channel_id=1, source_target_pairs={{0,1},{1,2},{2,3},{3,4},{4,5},{5,6},{6,7},{7,0},{8,9},{9,10},{10,1... | collective-permute-start | bytes 245768 | tf_op jit(solution)/shard_map/ppermute | solution.py:639
  14.3 0.0 copy-done
  14.3 0.6 %fusion = (s32[1]{0:T(128)}, s32[1]{0:T(128)}) fusion(s32[4]{0:T(128)S(1)} %copy-done), kind=kLoop, calls=%fused_computation.10 | loop fusion | bytes 16 | tf_op jit(solution)/shard_map/slice | solution.py:805
  16.2 0.0 slice-done
  16.2 0.0 slice-done.1
  16.2 1.0 %moments.1 = (f32[2,4,16,512]{3,2,1,0:T(8,128)S(1)}, f32[2,14,8,512]{3,2,1,0:T(8,128)S(1)}, f32[2,8,128]{2,1,0:T(8,128)S(1)}) custom-call(f32[40,512]{1,0:T(8,128)S(1)} %constant_dynamic-update-slice_fusion.after_north, f32[40,512]{1,0:T(8,128)S(1)} %constant_dynamic-update-slice_fusion.2.after_south, s32[4]{0:T(128)S(1)} %copy-done, ...), custom_call_target="tpu_custom_call" | custom-call | tf_op jit(solution)/shard_map/moments/pallas_call | solution.py:686
  17.1 0.0 collective-permute-done.31.north_msg
  17.2 0.0 collective-permute-done.30.south_msg
  17.2 1.6 %faces.1 = (f32[10,24,512]{2,1,0:T(8,128)S(1)}, f32[10,16,512]{2,1,0:T(8,128)S(1)}, f32[10,8,512]{2,1,0:T(8,128)S(1)}, f32[10,16,512]{2,1,0:T(8,128)S(1)}, f32[1...) custom-call(f32[2,8,128]{2,1,0:T(8,128)S(1)} %get-tuple-element.223., ...), custom_call_target="tpu_custom_call" | custom-call | tf_op jit(solution)/shard_map/faces/pallas_call | solution.py:705
  18.7 37.9 %conditional.1 = ((f32[19,8,16,512]{3,2,1,0:T(8,128)}, f32[19,8,16,512]{3,2,1,0:T(8,128)})) conditional(s32[]{:T(128)} %bitcast, (f32[10,8,512]{2,1,0:T(8,128)S(1)}, f32[10,16,512]{2,1,0:T(8,128)S(1)}, f32[10,8,512]{2,1,0:T(8,128)S(1)}, f32[10,16,512]{2,1,0:T(8,128)S(1)}, f32[104,512]{1,0:T(8,128)S(1)}, ...), branch_computations={%region_2.0_spmd, %region_3.0_spmd, %region_4.0_spmd, %region_5.0_... | conditional | flops 81920 | bytes 9044256 | solution.py:810
  18.8 1.6 %collective-permute-start.26 = (f32[10,24,512]{2,1,0:T(8,128)S(1)}, f32[10,24,512]{2,1,0:T(8,128)S(1)}, u32[]{:S(2)}, u32[]{:S(2)}) collective-permute-start(f32[10,24,512]{2,1,0:T(8,128)S(1)} %get-tuple-element.191), channel_id=1, source_target_pairs={{0,1},{1,0},{2,3},{3,2},{4,5},{5,4},{6,7},{7,6},{8,9},{9,8},{10,11... | collective-permute-start | bytes 1474568 | tf_op jit(solution)/shard_map/cond/branch_3_fun/ppermute | solution.py:639
  20.4 0.0 collective-permute-start.21
  20.4 1.5 %collective-permute-done.26.mate_rim = f32[10,24,512]{2,1,0:T(8,128)S(1)} collective-permute-done((f32[10,24,512]{2,1,0:T(8,128)S(1)}, f32[10,24,512]{2,1,0:T(8,128)S(1)}, u32[]{:S(2)}, u32[]{:S(2)}) %collective-permute-start.26) | collective-permute-done | bytes 491552 | tf_op jit(solution)/shard_map/cond/branch_3_fun/ppermute | solution.py:639
  21.9 0.1 collective-permute-start.27
  22.0 5.5 %collective-permute-done.21.cross_rim = f32[10,8,512]{2,1,0:T(8,128)S(1)} collective-permute-done((f32[10,8,512]{2,1,0:T(8,128)S(1)}, f32[10,8,512]{2,1,0:T(8,128)S(1)}, u32[]{:S(2)}, u32[]{:S(2)}) %collective-permute-start.21) | collective-permute-done | bytes 163872 | tf_op jit(solution)/shard_map/cond/branch_3_fun/ppermute | solution.py:639
  27.5 0.7 %collective-permute-start.22 = (f32[10,16,512]{2,1,0:T(8,128)S(1)}, f32[10,16,512]{2,1,0:T(8,128)S(1)}, u32[]{:S(2)}, u32[]{:S(2)}) collective-permute-start(f32[10,16,512]{2,1,0:T(8,128)S(1)} %get-tuple-element.186), channel_id=1, source_target_pairs={{0,28},{2,30},{4,24},{6,26},{25,5},{27,7},{29,1},{31,3}} | collective-permute-start | bytes 983048 | tf_op jit(solution)/shard_map/cond/branch_3_fun/ppermute | solution.py:755
  28.2 5.7 %collective-permute-start.24 = (f32[10,16,512]{2,1,0:T(8,128)S(1)}, f32[10,16,512]{2,1,0:T(8,128)S(1)}, u32[]{:S(2)}, u32[]{:S(2)}) collective-permute-start(f32[10,16,512]{2,1,0:T(8,128)S(1)} %get-tuple-element.188), channel_id=1, source_target_pairs={{0,11},{2,13},{4,15},{6,9},{8,19},{9,6},{10,21},{11,0},{12,23},{13... | collective-permute-start | bytes 983048 | tf_op jit(solution)/shard_map/cond/branch_3_fun/ppermute | solution.py:755
  33.8 0.7 %collective-permute-start.25 = (f32[104,512]{1,0:T(8,128)S(1)}, f32[104,512]{1,0:T(8,128)S(1)}, u32[]{:S(2)}, u32[]{:S(2)}) collective-permute-start(f32[104,512]{1,0:T(8,128)S(1)} %get-tuple-element.189), channel_id=1, source_target_pairs={{1,30},{3,24},{5,26},{7,28},{24,3},{26,5},{28,7},{30,1}} | collective-permute-start | bytes 638984 | tf_op jit(solution)/shard_map/cond/branch_3_fun/ppermute | solution.py:755
  34.5 1.9 %collective-permute-start.23 = (f32[10,8,512]{2,1,0:T(8,128)S(1)}, f32[10,8,512]{2,1,0:T(8,128)S(1)}, u32[]{:S(2)}, u32[]{:S(2)}) collective-permute-start(f32[10,8,512]{2,1,0:T(8,128)S(1)} %get-tuple-element.187), channel_id=1, source_target_pairs={{1,13},{3,15},{5,9},{7,11},{8,4},{9,21},{10,6},{11,23},{12,0},{13,... | collective-permute-start | bytes 491528 | tf_op jit(solution)/shard_map/cond/branch_3_fun/ppermute | solution.py:755
  36.4 8.9 %bulk.7 = (f32[19,8,16,512]{3,2,1,0:T(8,128)}, f32[19,8,16,512]{3,2,1,0:T(8,128)}) custom-call(f32[10,16,512]{2,1,0:T(8,128)S(1)} %slice_add_fusion.3.after, f32[19,8,16,512]{3,2,1,0:T(8,128)S(1)} %get-tuple-element.192.f_ref, f32[19,8,16,512]{3,2,1,0:T(8,128)S(1)} %get-tuple-element.193.g_ref, f32[8,16,512]{2,1,0:T(8,128)S(1)} %get-tuple-element.194.phi_ref, ...), custom_call_target="tpu_custom_call" | custom-call | tf_op jit(solution)/shard_map/cond/branch_3_fun/bulk/pallas_call | solution.py:770
  45.3 2.5 %collective-permute-done.27.joint = f32[10,16,512]{2,1,0:T(8,128)S(1)} collective-permute-done((f32[10,16,512]{2,1,0:T(8,128)S(1)}, f32[10,16,512]{2,1,0:T(8,128)S(1)}, u32[]{:S(2)}, u32[]{:S(2)}) %collective-permute-start.27) | collective-permute-done | bytes 327712 | tf_op jit(solution)/shard_map/cond/branch_3_fun/ppermute | solution.py:639
  47.8 0.8 %joint_fill.7 = (f32[19,8,16,512]{3,2,1,0:T(8,128)}, f32[19,8,16,512]{3,2,1,0:T(8,128)}) custom-call(f32[10,16,512]{2,1,0:T(8,128)S(1)} %collective-permute-done.27.joint, f32[19,8,16,512]{3,2,1,0:T(8,128)} %get-tuple-element.200.f_in, f32[19,8,16,512]{3,2,1,0:T(8,128)} %get-tuple-element.201.g_in), custom_call_target="tpu_custom_call", output_to_operand_aliasing={{0}: (1, {}), {1}: (2, {})} | custom-call | tf_op jit(solution)/shard_map/cond/branch_3_fun/joint_fill/pallas_call | solution.py:783
  48.6 7.2 %collective-permute-done.23.direct_short = f32[10,8,512]{2,1,0:T(8,128)S(1)} collective-permute-done((f32[10,8,512]{2,1,0:T(8,128)S(1)}, f32[10,8,512]{2,1,0:T(8,128)S(1)}, u32[]{:S(2)}, u32[]{:S(2)}) %collective-permute-start.23) | collective-permute-done | bytes 163872 | tf_op jit(solution)/shard_map/cond/branch_3_fun/ppermute | solution.py:755
  55.8 0.0 collective-permute-done.25.across_short
  55.8 0.0 collective-permute-done.22.direct
  55.8 0.0 collective-permute-done.24.across
  55.8 0.8 %merge_fill.7 = (f32[19,8,16,512]{3,2,1,0:T(8,128)}, f32[19,8,16,512]{3,2,1,0:T(8,128)}) custom-call(f32[10,16,512]{2,1,0:T(8,128)S(1)} %collective-permute-done.22.direct, f32[10,8,512]{2,1,0:T(8,128)S(1)} %collective-permute-done.23.direct_short, f32[10,16,512]{2,1,0:T(8,128)S(1)} %collective-permute-done.24.across, ...), custom_call_target="tpu_custom_call", output_to_operand_aliasing={{0}: (4, {}), {1}: (5, {})} | custom-call | tf_op jit(solution)/shard_map/cond/branch_3_fun/merge_fill/pallas_call | solution.py:794
  (7 shorter events, 0.1 us)
Async XLA Ops:
  0.6 4.8 %copy-start.1 = (f32[19,8,16,512]{3,2,1,0:T(8,128)S(1)}, f32[19,8,16,512]{3,2,1,0:T(8,128)}, u32[]{:S(2)}) copy-start(f32[19,8,16,512]{3,2,1,0:T(8,128)} %g_ref.7) | copy-start | bytes 14942212
  2.2 4.8 %collective-permute-start.29 = (f32[16,512]{1,0:T(8,128)S(1)}, f32[16,512]{1,0:T(8,128)S(1)}, u32[]{:S(2)}, u32[]{:S(2)}) collective-permute-start(f32[16,512]{1,0:T(8,128)S(1)} %get-tuple-element.246.top), channel_id=1, source_target_pairs={{0,12},{1,13},{2,14},{3,15},{4,8},{5,9},{6,10},{7,11},{8,20},{9,21... | collective-permute-start | bytes 98312 | tf_op jit(solution)/shard_map/ppermute | solution.py:639
  5.4 5.5 %collective-permute-start.28 = (f32[16,512]{1,0:T(8,128)S(1)}, f32[16,512]{1,0:T(8,128)S(1)}, u32[]{:S(2)}, u32[]{:S(2)}) collective-permute-start(f32[16,512]{1,0:T(8,128)S(1)} %get-tuple-element.247.bottom), channel_id=1, source_target_pairs={{0,28},{1,29},{2,30},{3,31},{4,24},{5,25},{6,26},{7,27},{8,4},{9,5... | collective-permute-start | bytes 98312 | tf_op jit(solution)/shard_map/ppermute | solution.py:639
  5.5 10.7 %slice-start = ((s8[4980736]{0:T(1024)(128)(4,1)}), s8[4194304]{0:T(1024)(128)(4,1)S(1)}, s32[]{:S(2)}) async-start(s8[4980736]{0:T(1024)(128)(4,1)} %bitcast.1), calls=%async_computation | async-start | bytes 8388608
  5.5 8.8 %copy-start = (s32[4]{0:T(128)S(1)}, s32[4]{0:T(128)}, u32[]{:S(2)}) copy-start(s32[4]{0:T(128)} %offsets.1) | copy-start | bytes 52
  5.5 10.7 %slice-start.1 = ((s8[4980736]{0:T(1024)(128)(4,1)}), s8[786432]{0:T(1024)(128)(4,1)S(1)}, s32[]{:S(2)}) async-start(s8[4980736]{0:T(1024)(128)(4,1)} %bitcast.1), calls=%async_computation.1 | async-start | bytes 1572864
  7.0 10.1 %collective-permute-start.31 = (f32[40,512]{1,0:T(8,128)S(1)}, f32[40,512]{1,0:T(8,128)S(1)}, u32[]{:S(2)}, u32[]{:S(2)}) collective-permute-start(f32[40,512]{1,0:T(8,128)S(1)} %constant_dynamic-update-slice_fusion.2.after_south), channel_id=1, source_target_pairs={{0,7},{1,0},{2,1},{3,2},{4,3},{5,4},{6,5},{7,6},{8,15},{9,8},{10,9... | collective-permute-start | bytes 245768 | tf_op jit(solution)/shard_map/ppermute | solution.py:639
  10.9 6.2 %collective-permute-start.30 = (f32[40,512]{1,0:T(8,128)S(1)}, f32[40,512]{1,0:T(8,128)S(1)}, u32[]{:S(2)}, u32[]{:S(2)}) collective-permute-start(f32[40,512]{1,0:T(8,128)S(1)} %constant_dynamic-update-slice_fusion.after_north), channel_id=1, source_target_pairs={{0,1},{1,2},{2,3},{3,4},{4,5},{5,6},{6,7},{7,0},{8,9},{9,10},{10,1... | collective-permute-start | bytes 245768 | tf_op jit(solution)/shard_map/ppermute | solution.py:639
  18.8 3.1 %collective-permute-start.26 = (f32[10,24,512]{2,1,0:T(8,128)S(1)}, f32[10,24,512]{2,1,0:T(8,128)S(1)}, u32[]{:S(2)}, u32[]{:S(2)}) collective-permute-start(f32[10,24,512]{2,1,0:T(8,128)S(1)} %get-tuple-element.191), channel_id=1, source_target_pairs={{0,1},{1,0},{2,3},{3,2},{4,5},{5,4},{6,7},{7,6},{8,9},{9,8},{10,11... | collective-permute-start | bytes 1474568 | tf_op jit(solution)/shard_map/cond/branch_3_fun/ppermute | solution.py:639
  20.4 7.1 %collective-permute-start.21 = (f32[10,8,512]{2,1,0:T(8,128)S(1)}, f32[10,8,512]{2,1,0:T(8,128)S(1)}, u32[]{:S(2)}, u32[]{:S(2)}) collective-permute-start(f32[10,8,512]{2,1,0:T(8,128)S(1)} %get-tuple-element.185), channel_id=1, source_target_pairs={{0,7},{1,2},{2,1},{3,4},{4,3},{5,6},{6,5},{7,0},{8,15},{9,10},{10,... | collective-permute-start | bytes 491528 | tf_op jit(solution)/shard_map/cond/branch_3_fun/ppermute | solution.py:639
  21.9 25.9 %collective-permute-start.27 = (f32[10,16,512]{2,1,0:T(8,128)S(1)}, f32[10,16,512]{2,1,0:T(8,128)S(1)}, u32[]{:S(2)}, u32[]{:S(2)}) collective-permute-start(f32[10,16,512]{2,1,0:T(8,128)S(1)} %slice_add_fusion.3.after), channel_id=1, source_target_pairs={{0,12},{1,29},{2,14},{3,31},{4,8},{5,25},{6,10},{7,27},{8,20},{9,5... | collective-permute-start | bytes 983048 | tf_op jit(solution)/shard_map/cond/branch_3_fun/ppermute | solution.py:639
  27.5 28.3 %collective-permute-start.22 = (f32[10,16,512]{2,1,0:T(8,128)S(1)}, f32[10,16,512]{2,1,0:T(8,128)S(1)}, u32[]{:S(2)}, u32[]{:S(2)}) collective-permute-start(f32[10,16,512]{2,1,0:T(8,128)S(1)} %get-tuple-element.186), channel_id=1, source_target_pairs={{0,28},{2,30},{4,24},{6,26},{25,5},{27,7},{29,1},{31,3}} | collective-permute-start | bytes 983048 | tf_op jit(solution)/shard_map/cond/branch_3_fun/ppermute | solution.py:755
  28.2 27.7 %collective-permute-start.24 = (f32[10,16,512]{2,1,0:T(8,128)S(1)}, f32[10,16,512]{2,1,0:T(8,128)S(1)}, u32[]{:S(2)}, u32[]{:S(2)}) collective-permute-start(f32[10,16,512]{2,1,0:T(8,128)S(1)} %get-tuple-element.188), channel_id=1, source_target_pairs={{0,11},{2,13},{4,15},{6,9},{8,19},{9,6},{10,21},{11,0},{12,23},{13... | collective-permute-start | bytes 983048 | tf_op jit(solution)/shard_map/cond/branch_3_fun/ppermute | solution.py:755
  33.8 22.0 %collective-permute-start.25 = (f32[104,512]{1,0:T(8,128)S(1)}, f32[104,512]{1,0:T(8,128)S(1)}, u32[]{:S(2)}, u32[]{:S(2)}) collective-permute-start(f32[104,512]{1,0:T(8,128)S(1)} %get-tuple-element.189), channel_id=1, source_target_pairs={{1,30},{3,24},{5,26},{7,28},{24,3},{26,5},{28,7},{30,1}} | collective-permute-start | bytes 638984 | tf_op jit(solution)/shard_map/cond/branch_3_fun/ppermute | solution.py:755
  34.5 21.3 %collective-permute-start.23 = (f32[10,8,512]{2,1,0:T(8,128)S(1)}, f32[10,8,512]{2,1,0:T(8,128)S(1)}, u32[]{:S(2)}, u32[]{:S(2)}) collective-permute-start(f32[10,8,512]{2,1,0:T(8,128)S(1)} %get-tuple-element.187), channel_id=1, source_target_pairs={{1,13},{3,15},{5,9},{7,11},{8,4},{9,21},{10,6},{11,23},{12,0},{13,... | collective-permute-start | bytes 491528 | tf_op jit(solution)/shard_map/cond/branch_3_fun/ppermute | solution.py:755

commit v2 on v1

--- a/solution.py
+++ b/solution.py
@@ -294,12 +294,78 @@
             rims[s, 9 + j] = g_ref[i, :, edge, :]
 
 
-def half_rows(rows, first):
-    return slice(0, rows // 2) if first else slice(rows // 2, rows)
-
-
-def seam_rows(rows, up):
-    return slice(rows // 2 - 2, rows // 2) if up else slice(rows // 2, rows // 2 + 2)
+displacement_classes = ((0, 5), (6, 10), (11, 15))
+
+
+def rows_needed(rest, rows):
+    return min(rows, rows + 1 - rest), min(rows, rest + 2)
+
+
+def message_rows(count, rows):
+    if count >= rows:
+        return 10 * rows
+    half = rows // 2
+    full = half if count >= half else 0
+    return 10 * full + -(-10 * (count - full) // 8) * 8
+
+
+def split_sizes(first, second, rows):
+    groups = [(0, 0), displacement_classes[first], displacement_classes[second], (rows - 1, rows - 1)]
+    direct = [max(rows_needed(r, rows)[0] for r in range(low, high + 1)) for low, high in groups]
+    across = [max(rows_needed(r, rows)[1] for r in range(low, high + 1)) for low, high in groups]
+
+    def options(needs):
+        for mask in range(16):
+            small = [k for k in range(4) if mask >> k & 1]
+            size = max([needs[k] for k in small], default=0)
+            if size < rows:
+                yield size, small
+
+    best = None
+    for d_size, d_small in options(direct):
+        for a_size, a_small in options(across):
+            costs = []
+            for k in range(4):
+                d_rows = message_rows(d_size if k in d_small else rows, rows)
+                a_rows = message_rows(a_size if k in a_small else rows, rows)
+                costs.append(2 * d_rows + a_rows)
+            pairs = [costs[k] + costs[(k + 1) % 4] for k in range(4)]
+            rank = (max(pairs), sum(pairs), d_size, a_size, d_small, a_small)
+            if best is None or rank < best:
+                best = rank
+    return best[2], best[4], best[3], best[5]
+
+
+def pieces(count, rows, first):
+    half = rows // 2
+    if count >= half:
+        tile = slice(0, half) if first else slice(half, rows)
+        rest = slice(half, count) if first else slice(rows - count, half)
+    else:
+        tile = None
+        rest = slice(0, count) if first else slice(rows - count, rows)
+    length = rest.stop - rest.start
+    base = 10 * half if tile else 0
+    places = []
+    if tile:
+        places.append((tile, lambda j: slice(half * j, half * j + half)))
+    if length:
+        places.append((rest, lambda j: slice(base + length * j, base + length * j + length)))
+    return places, base + 10 * length
+
+
+def pack(out, source, count, rows, first):
+    places, used = pieces(count, rows, first)
+    for j in range(10):
+        for window, place in places:
+            out[place(j)] = source[j, window]
+    if used < out.shape[0]:
+        out[used:] = jnp.zeros((out.shape[0] - used, out.shape[1]), f32)
+
+
+def unpack_add(buf, j, message, count, rows, first):
+    for window, place in pieces(count, rows, first)[0]:
+        buf[j, window] = buf[j, window] + message[place(j)]
 
 
 def rim_values(rims, s, phi_ref, minus, plus, south_msg, north_msg, line, edge, chosen, out):
@@ -328,6 +394,7 @@
 
 def face_kernel(
     count_x,
+    sizes,
     rests,
     f_ref,
     g_ref,
@@ -429,9 +496,6 @@
                 value = even + odd - (1.0 / 9.0) * g_ref[i, x, span] + phi_h * change
                 post[side, 5 + j, span] = z_moved(value, cz)
 
-    part = rows // 2
-    seam = 10 * part
-
     def hand_out(is_odd):
         for side, up in enumerate((True, False)):
             if up:
@@ -457,10 +521,8 @@
         for j in range(10):
             mate[j, rows : rows + layers] = rim_post[1 if is_odd else 0, j]
             cross[j] = rim_post[0 if is_odd else 1, j]
-            direct_short[j] = direct[j, half_rows(rows, is_odd)]
-            across_short[part * j : part * j + part] = across[j, half_rows(rows, is_odd)]
-            across_short[seam + 2 * j : seam + 2 * j + 2] = across[j, seam_rows(rows, not is_odd)]
-        across_short[seam + 20 : seam + 24] = jnp.zeros((4, cols), f32)
+        pack(direct_short, direct, sizes[0], rows, is_odd)
+        pack(across_short, across, sizes[1], rows, is_odd)
 
     pl.when(planes.odd)(lambda: hand_out(True))
     pl.when(jnp.logical_not(planes.odd))(lambda: hand_out(False))
@@ -561,7 +623,7 @@
 
 def merge_fill_kernel(
     count_x,
-    long_planes,
+    split,
     direct,
     direct_short,
     across,
@@ -574,13 +636,11 @@
     sems,
 ):
     layers, rows = f_out.shape[1], f_out.shape[2]
+    d_size, d_small, a_size, a_small = split
     a = lax.axis_index("gx")
     odd = lax.rem(lax.axis_index("gy"), 2) == 1
-    part = rows // 2
-    seam = 10 * part
 
     def merge(column, up):
-        near, other, between = half_rows(rows, up), half_rows(rows, not up), seam_rows(rows, up)
         chosen, x = (rising, 0) if up else (falling, layers - 1)
         copies = [
             pltpu.make_async_copy(
@@ -589,27 +649,31 @@
             for j in range(10)
         ]
 
-        def long():
+        def fill(short_direct, short_across):
             for j in range(10):
-                buf[j, near] = across[j, near] + direct_short[j]
-                buf[j, other] = across[j, other]
+                if short_direct and short_across:
+                    buf[j] = jnp.zeros(buf.shape[1:], f32)
+                elif short_direct:
+                    buf[j] = across[j]
+                elif short_across:
+                    buf[j] = direct[j]
+                else:
+                    buf[j] = direct[j] + across[j]
+                if short_direct:
+                    unpack_add(buf, j, direct_short, d_size, rows, up)
+                if short_across:
+                    unpack_add(buf, j, across_short, a_size, rows, not up)
                 copies[j].start()
 
-        def short():
-            for j in range(10):
-                at = seam + 2 * j
-                buf[j, near] = direct[j, near]
-                buf[j, between] = direct[j, between] + across_short[at : at + 2]
-                buf[j, other] = direct[j, other] + across_short[part * j : part * j + part]
-                copies[j].start()
-
         is_plane, plane = plane_at(column, count_x)
-        in_set = plane == long_planes[0]
-        for k in long_planes[1:]:
-            in_set = jnp.logical_or(in_set, plane == k)
-        is_long = jnp.logical_and(is_plane, in_set)
-        pl.when(is_long)(long)
-        pl.when(jnp.logical_not(is_long))(short)
+        plane = jnp.where(is_plane, plane, 0)
+        modes = [(k in d_small, k in a_small) for k in range(4)]
+        for mode in sorted(set(modes)):
+            members = [k for k in range(4) if modes[k] == mode]
+            inside = plane == members[0]
+            for k in members[1:]:
+                inside = jnp.logical_or(inside, plane == k)
+            pl.when(inside)(functools.partial(fill, *mode))
         for copy in copies:
             copy.wait()
 
@@ -696,73 +760,74 @@
         name="moments",
     )(to_north, to_south, offsets, momentum_dist, order_dist)
 
-    part = rows // 2
     ten = jax.ShapeDtypeStruct((10, rows, cols), f32)
-    ten_short = jax.ShapeDtypeStruct((10, part, cols), f32)
-    ten_seam = jax.ShapeDtypeStruct((10 * part + 24, cols), f32)
     side = jax.ShapeDtypeStruct((10, layers, cols), f32)
     ten_side = jax.ShapeDtypeStruct((10, rows + layers, cols), f32)
-    *outgoing, minus, plus = pl.pallas_call(
-        functools.partial(face_kernel, count_x),
-        out_shape=[ten_side, ten, ten_short, ten, ten_seam, ten, side] + [plane] * 2,
-        in_specs=[vmem] * 10,
-        out_specs=[vmem] * 9,
-        scratch_shapes=[
-            VMEM((rows + 16, cols), f32),
-            VMEM((rows + 16, cols), f32),
-            VMEM((cols // LANES, 2 * rows + 16, LANES), f32),
-            VMEM((rows + 16, cols), f32),
-            VMEM((layers + 16, cols), f32),
-            VMEM((2, 10, layers, cols), f32),
-            VMEM((2, 10, rows, cols), f32),
-            VMEM((11, 8, cols), f32),
-            VMEM((2, 8, cols), f32),
-            VMEM((cols // LANES, rows + 16, LANES), f32),
-            VMEM((cols // LANES, 3 * rows + 16, LANES), f32),
-        ],
-        compiler_params=params(24 << 20),
-        name="faces",
-    )(
-        rests,
-        momentum_dist,
-        order_dist,
-        face_moments,
-        rims,
-        phi,
-        rise,
-        fall,
-        south_msg,
-        north_msg,
-    )
-    around = (phi, minus, plus, south_msg, north_msg)
     whole = jax.ShapeDtypeStruct(momentum_dist.shape, f32)
 
-    def finish(long_planes, mate, direct, direct_short, across, across_short, joint, cross):
-
-        def is_long(x):
-            return x % per_plane == 0 and x // per_plane % 4 in long_planes
-
-        def hop_some(value, odd_up, extra, long):
+    def finish(first, second):
+        split = split_sizes(first, second, rows)
+        d_size, d_small, a_size, a_small = split
+        d_short = jax.ShapeDtypeStruct((max(8, message_rows(d_size, rows)), cols), f32)
+        a_short = jax.ShapeDtypeStruct((max(8, message_rows(a_size, rows)), cols), f32)
+
+        def hop_some(value, odd_up, extra, planes):
             pairs = []
             for x in range(count_x):
                 for y in range(count_y):
                     up = (y % 2 == 1) == odd_up
                     tx = (x + 1 if up else x - 1) % count_x
-                    if is_long(tx if up else x) != long:
+                    column = tx if up else x
+                    if (column // per_plane % 4 if column % per_plane == 0 else 0) not in planes:
                         continue
                     ty = y - base_up(x) - extra if up else y + base_low(x) + extra
                     pairs.append((x * count_y + y, tx * count_y + ty % count_y))
-            return lax.ppermute(value, ("gx", "gy"), pairs)
-
+            return lax.ppermute(value, ("gx", "gy"), pairs) if pairs else value
+
+        mate, direct, direct_short, across, across_short, joint, cross, minus, plus = pl.pallas_call(
+            functools.partial(face_kernel, count_x, (d_size, a_size)),
+            out_shape=[ten_side, ten, d_short, ten, a_short, ten, side] + [plane] * 2,
+            in_specs=[vmem] * 10,
+            out_specs=[vmem] * 9,
+            scratch_shapes=[
+                VMEM((rows + 16, cols), f32),
+                VMEM((rows + 16, cols), f32),
+                VMEM((cols // LANES, 2 * rows + 16, LANES), f32),
+                VMEM((rows + 16, cols), f32),
+                VMEM((layers + 16, cols), f32),
+                VMEM((2, 10, layers, cols), f32),
+                VMEM((2, 10, rows, cols), f32),
+                VMEM((11, 8, cols), f32),
+                VMEM((2, 8, cols), f32),
+                VMEM((cols // LANES, rows + 16, LANES), f32),
+                VMEM((cols // LANES, 3 * rows + 16, LANES), f32),
+            ],
+            compiler_params=params(24 << 20),
+            name="faces",
+        )(
+            rests,
+            momentum_dist,
+            order_dist,
+            face_moments,
+            rims,
+            phi,
+            rise,
+            fall,
+            south_msg,
+            north_msg,
+        )
+        around = (phi, minus, plus, south_msg, north_msg)
         cross = hop(cross, lambda x, y: (x, y + 1 if y % 2 == 1 else y - 1))
         mate = hop(mate, lambda x, y: (x, y ^ 1))
         direct, direct_short, across, across_short, cross = lax.optimization_barrier(
             (direct, direct_short, across, across_short, cross)
         )
-        direct = hop_some(direct, True, 0, False)
-        direct_short = hop_some(direct_short, True, 0, True)
-        across = hop_some(across, False, 1, True)
-        across_short = hop_some(across_short, False, 1, False)
+        d_full = [k for k in range(4) if k not in d_small]
+        a_full = [k for k in range(4) if k not in a_small]
+        direct = hop_some(direct, True, 0, d_full)
+        direct_short = hop_some(direct_short, True, 0, d_small)
+        across = hop_some(across, False, 1, a_full)
+        across_short = hop_some(across_short, False, 1, a_small)
         joint = joint + mate[:, :rows]
         after = joint
         joint = hop_parity(joint, False, 0)
@@ -792,7 +857,7 @@
         )(joint, next_f, next_g)
 
         return pl.pallas_call(
-            functools.partial(merge_fill_kernel, count_x, sorted(long_planes)),
+            functools.partial(merge_fill_kernel, count_x, split),
             out_shape=[whole, whole],
             in_specs=[vmem] * 4 + [anywhere, anywhere],
             out_specs=[anywhere, anywhere],
@@ -802,12 +867,13 @@
             name="merge_fill",
         )(direct, direct_short, across, across_short, next_f, next_g)
 
-    is_long = [(offsets[k] - half * rows > part).astype(jnp.int32) for k in (1, 2)]
-    branches = [
-        functools.partial(finish, {3} | ({1} if k & 2 else set()) | ({2} if k & 1 else set()))
-        for k in range(4)
+    edges = [high for _, high in displacement_classes[:-1]]
+    kinds = [
+        sum((offsets[k] - half * rows > edge).astype(jnp.int32) for edge in edges) for k in (1, 2)
     ]
-    return lax.switch(2 * is_long[0] + is_long[1], branches, *outgoing)
+    count = len(displacement_classes)
+    branches = [functools.partial(finish, k // count, k % count) for k in range(count * count)]
+    return lax.switch(count * kinds[0] + kinds[1], branches)
 
 
 def solution(mesh):

time: 57.2 us -> 60.4 us (1.056)
  the two profiles are of different devices: /device:TPU:3 before, /device:TPU:0 now
where the time goes in v2:
time: 60.4 us; the launch traced here: 60.9 us
  starting transfers between devices  25.5 us (42%)
  Pallas kernels  16.9 us (28%)
  waiting for transfers between devices  13.5 us (22%)
  between operations  2.26 us (4%)
  other arithmetic  1.55 us (3%)
  local copies, waits for them, and re-layouts  0.63 us (1%)
  loops' own time  0.62 us (1%)
    ppermute x4, starting transfers between devices, hop_some(): return lax.ppermute(value, ('gx', 'gy'), pairs) if pairs else value  14.7 us
    pallas_call x1, Pallas kernels, finish(): pl.pallas_call(bulk_kernel, out_shape=[whole, whole], in_specs=[anywhere]...  11.3 us
    ppermute x7, starting transfers between devices, hop(): return lax.ppermute(value, ('gx', 'gy'), perm)  10.8 us
    ppermute x7, waiting for transfers between devices, hop(): return lax.ppermute(value, ('gx', 'gy'), perm)  7.96 us
    ppermute x4, waiting for transfers between devices, hop_some(): return lax.ppermute(value, ('gx', 'gy'), pairs) if pairs else value  5.51 us
    pallas_call x1, Pallas kernels, finish(): pl.pallas_call(functools.partial(face_kernel, count_x, (d_size, a_size)),...  1.54 us
    reduce_sum x1, other arithmetic, on_device(): jnp.sum(order_dist[:, layers - 1], axis=0)  1.51 us
    pallas_call x1, Pallas kernels, on_device(): pl.pallas_call(phi_kernel, out_shape=[jax.ShapeDtypeStruct((layers, rows,...  1.47 us
  transfers between devices with their start and end apart: 11, of which 6 were waited for; matrix products, arithmetic and copies ran while one was open for 1% of the time, Pallas kernels for 24%

profile of v2, /device:TPU:0, one launch (start us, length us, event | category | flops | bytes accessed | tf_op | source)
XLA Modules:
  0.0 60.9 jit_solution(3120451889302100053)
XLA Ops:
  0.6 0.0 copy-start.1
  0.6 1.5 %slice_reduce_fusion = (f32[16,512]{1,0:T(8,128)S(1)}, f32[16,512]{1,0:T(8,128)S(1)}) fusion(f32[19,8,16,512]{3,2,1,0:T(8,128)} %g_ref.5), kind=kLoop, calls=%fused_computation.9 | loop fusion | flops 294912 | bytes 1310720 | tf_op jit(solution)/shard_map/reduce_sum | solution.py:724
  2.2 5.0 %collective-permute-start.64 = (f32[16,512]{1,0:T(8,128)S(1)}, f32[16,512]{1,0:T(8,128)S(1)}, u32[]{:S(2)}, u32[]{:S(2)}) collective-permute-start(f32[16,512]{1,0:T(8,128)S(1)} %get-tuple-element.466.top), channel_id=1, source_target_pairs={{0,12},{1,13},{2,14},{3,15},{4,8},{5,9},{6,10},{7,11},{8,20},{9,21... | collective-permute-start | bytes 98312 | tf_op jit(solution)/shard_map/ppermute | solution.py:703
  7.2 1.0 %collective-permute-start.63 = (f32[16,512]{1,0:T(8,128)S(1)}, f32[16,512]{1,0:T(8,128)S(1)}, u32[]{:S(2)}, u32[]{:S(2)}) collective-permute-start(f32[16,512]{1,0:T(8,128)S(1)} %get-tuple-element.467.bottom), channel_id=1, source_target_pairs={{0,28},{1,29},{2,30},{3,31},{4,24},{5,25},{6,26},{7,27},{8,4},{9,5... | collective-permute-start | bytes 98312 | tf_op jit(solution)/shard_map/ppermute | solution.py:703
  8.2 0.0 slice-start
  8.2 0.0 copy-done.1
  8.2 0.0 copy-start
  8.2 0.0 slice-start.1
  8.2 1.5 %phi_all.1 = (f32[8,16,512]{2,1,0:T(8,128)S(1)}, f32[24,512]{1,0:T(8,128)S(1)}, f32[24,512]{1,0:T(8,128)S(1)}) custom-call(f32[8,128]{1,0:T(8,128)S(1)} %gate.1, f32[19,8,16,512]{3,2,1,0:T(8,128)} %f_ref.3, f32[19,8,16,512]{3,2,1,0:T(8,128)S(1)} %copy-done.1, f32[16,512]{1,0:T(8,128)S(1)} %get-tuple-element.466.top, f32[16,512]{1,0:T(8,128)S(1)} %get-tuple-element.467.bottom), custom_call_target="tpu_custom_call" | custom-call | tf_op jit(solution)/shard_map/phi_all/pallas_call | solution.py:737
  9.7 0.7 %collective-permute-done.64 = f32[16,512]{1,0:T(8,128)S(1)} collective-permute-done((f32[16,512]{1,0:T(8,128)S(1)}, f32[16,512]{1,0:T(8,128)S(1)}, u32[]{:S(2)}, u32[]{:S(2)}) %collective-permute-start.64) | collective-permute-done | bytes 32800 | tf_op jit(solution)/shard_map/ppermute | solution.py:703
  10.4 2.1 %collective-permute-start.66 = (f32[40,512]{1,0:T(8,128)S(1)}, f32[40,512]{1,0:T(8,128)S(1)}, u32[]{:S(2)}, u32[]{:S(2)}) collective-permute-start(f32[40,512]{1,0:T(8,128)S(1)} %constant_dynamic-update-slice_fusion.2.after_south), channel_id=1, source_target_pairs={{0,7},{1,0},{2,1},{3,2},{4,3},{5,4},{6,5},{7,6},{8,15},{9,8},{10,9... | collective-permute-start | bytes 245768 | tf_op jit(solution)/shard_map/ppermute | solution.py:703
  12.5 0.4 collective-permute-done.63
  12.9 0.1 collective-permute-start.65
  13.0 0.0 copy-done
  13.0 0.6 fusion
  14.9 0.0 slice-done
  14.9 0.0 slice-done.1
  14.9 1.0 %moments.1 = (f32[2,4,16,512]{3,2,1,0:T(8,128)S(1)}, f32[2,14,8,512]{3,2,1,0:T(8,128)S(1)}, f32[2,8,128]{2,1,0:T(8,128)S(1)}) custom-call(f32[40,512]{1,0:T(8,128)S(1)} %constant_dynamic-update-slice_fusion.after_north, f32[40,512]{1,0:T(8,128)S(1)} %constant_dynamic-update-slice_fusion.2.after_south, s32[4]{0:T(128)S(1)} %copy-done, ...), custom_call_target="tpu_custom_call" | custom-call | tf_op jit(solution)/shard_map/moments/pallas_call | solution.py:750
  15.9 0.0 collective-permute-done.66
  15.9 2.7 %collective-permute-done.65 = f32[40,512]{1,0:T(8,128)S(1)} collective-permute-done((f32[40,512]{1,0:T(8,128)S(1)}, f32[40,512]{1,0:T(8,128)S(1)}, u32[]{:S(2)}, u32[]{:S(2)}) %collective-permute-start.65) | collective-permute-done | bytes 81952 | tf_op jit(solution)/shard_map/ppermute | solution.py:703
  18.6 42.1 %conditional.1 = ((f32[19,8,16,512]{3,2,1,0:T(8,128)}, f32[19,8,16,512]{3,2,1,0:T(8,128)})) conditional(s32[]{:T(128)} %bitcast, (f32[2,8,128]{2,1,0:T(8,128)S(1)}, f32[19,8,16,512]{3,2,1,0:T(8,128)S(1)}, f32[19,8,16,512]{3,2,1,0:T(8,128)S(1)}, f32[2,4,16,512]{3,2,1,0:T(8,128)S(1)}, f32[2,14,8,512]{3,2,1,0:T(8,128)S(1)}, ...), branch_computations={%region_2.0_spmd, %region_3.0_spmd, %region_4.0_spmd, %region_5.0_... | conditional | flops 81920 | bytes 28967228 | solution.py:876
  18.6 0.0 copy-start.2
  18.6 1.5 %faces.10 = (f32[10,24,512]{2,1,0:T(8,128)S(1)}, f32[10,16,512]{2,1,0:T(8,128)S(1)}, f32[112,512]{1,0:T(8,128)S(1)}, f32[10,16,512]{2,1,0:T(8,128)S(1)}, f32[72,...) custom-call(f32[2,8,128]{2,1,0:T(8,128)S(1)} %get-tuple-element.208., ...), custom_call_target="tpu_custom_call" | custom-call | tf_op jit(solution)/shard_map/cond/branch_1_fun/faces/pallas_call | solution.py:787
  20.2 0.1 collective-permute-start.12
  20.2 1.2 %collective-permute-start.7 = (f32[10,8,512]{2,1,0:T(8,128)S(1)}, f32[10,8,512]{2,1,0:T(8,128)S(1)}, u32[]{:S(2)}, u32[]{:S(2)}) collective-permute-start(f32[10,8,512]{2,1,0:T(8,128)S(1)} %get-tuple-element.222), channel_id=1, source_target_pairs={{0,7},{1,2},{2,1},{3,4},{4,3},{5,6},{6,5},{7,0},{8,15},{9,10},{10,... | collective-permute-start | bytes 491528 | tf_op jit(solution)/shard_map/cond/branch_1_fun/ppermute | solution.py:703
  21.4 0.7 %collective-permute-done.12.mate_rim = f32[10,24,512]{2,1,0:T(8,128)S(1)} collective-permute-done((f32[10,24,512]{2,1,0:T(8,128)S(1)}, f32[10,24,512]{2,1,0:T(8,128)S(1)}, u32[]{:S(2)}, u32[]{:S(2)}) %collective-permute-start.12) | collective-permute-done | bytes 491552 | tf_op jit(solution)/shard_map/cond/branch_1_fun/ppermute | solution.py:703
  22.1 0.0 copy-done.2
  22.1 1.4 %collective-permute-start.13 = (f32[10,16,512]{2,1,0:T(8,128)S(1)}, f32[10,16,512]{2,1,0:T(8,128)S(1)}, u32[]{:S(2)}, u32[]{:S(2)}) collective-permute-start(f32[10,16,512]{2,1,0:T(8,128)S(1)} %slice_add_fusion.1.after), channel_id=1, source_target_pairs={{0,12},{1,29},{2,14},{3,31},{4,8},{5,25},{6,10},{7,27},{8,20},{9,5... | collective-permute-start | bytes 983048 | tf_op jit(solution)/shard_map/cond/branch_1_fun/ppermute | solution.py:703
  23.5 3.4 %collective-permute-done.7.cross_rim = f32[10,8,512]{2,1,0:T(8,128)S(1)} collective-permute-done((f32[10,8,512]{2,1,0:T(8,128)S(1)}, f32[10,8,512]{2,1,0:T(8,128)S(1)}, u32[]{:S(2)}, u32[]{:S(2)}) %collective-permute-start.7) | collective-permute-done | bytes 163872 | tf_op jit(solution)/shard_map/cond/branch_1_fun/ppermute | solution.py:703
  27.0 1.9 %collective-permute-start.8 = (f32[10,16,512]{2,1,0:T(8,128)S(1)}, f32[10,16,512]{2,1,0:T(8,128)S(1)}, u32[]{:S(2)}, u32[]{:S(2)}) collective-permute-start(f32[10,16,512]{2,1,0:T(8,128)S(1)} %get-tuple-element.223), channel_id=1, source_target_pairs={{0,28},{1,13},{2,30},{3,15},{4,24},{5,9},{6,26},{7,11},{8,4},{10,6... | collective-permute-start | bytes 983048 | tf_op jit(solution)/shard_map/cond/branch_1_fun/ppermute | solution.py:785
  28.9 0.7 %collective-permute-start.10 = (f32[10,16,512]{2,1,0:T(8,128)S(1)}, f32[10,16,512]{2,1,0:T(8,128)S(1)}, u32[]{:S(2)}, u32[]{:S(2)}) collective-permute-start(f32[10,16,512]{2,1,0:T(8,128)S(1)} %get-tuple-element.225), channel_id=1, source_target_pairs={{8,19},{10,21},{12,23},{14,17},{16,27},{17,14},{18,29},{19,8},{20,... | collective-permute-start | bytes 983048 | tf_op jit(solution)/shard_map/cond/branch_1_fun/ppermute | solution.py:785
  29.6 0.7 %collective-permute-start.9 = (f32[112,512]{1,0:T(8,128)S(1)}, f32[112,512]{1,0:T(8,128)S(1)}, u32[]{:S(2)}, u32[]{:S(2)}) collective-permute-start(f32[112,512]{1,0:T(8,128)S(1)} %get-tuple-element.224), channel_id=1, source_target_pairs={{9,21},{11,23},{13,17},{15,19},{16,12},{17,29},{18,14},{19,31},{20... | collective-permute-start | bytes 688136 | tf_op jit(solution)/shard_map/cond/branch_1_fun/ppermute | solution.py:785
  30.2 11.5 %collective-permute-start.11 = (f32[72,512]{1,0:T(8,128)S(1)}, f32[72,512]{1,0:T(8,128)S(1)}, u32[]{:S(2)}, u32[]{:S(2)}) collective-permute-start(f32[72,512]{1,0:T(8,128)S(1)} %get-tuple-element.226), channel_id=1, source_target_pairs={{0,11},{1,30},{2,13},{3,24},{4,15},{5,26},{6,9},{7,28},{9,6},{11,0... | collective-permute-start | bytes 442376 | tf_op jit(solution)/shard_map/cond/branch_1_fun/ppermute | solution.py:785
  41.7 11.3 %bulk.10 = (f32[19,8,16,512]{3,2,1,0:T(8,128)}, f32[19,8,16,512]{3,2,1,0:T(8,128)}) custom-call(f32[10,16,512]{2,1,0:T(8,128)S(1)} %slice_add_fusion.1.after, f32[19,8,16,512]{3,2,1,0:T(8,128)S(1)} %get-tuple-element.209.f_ref, f32[19,8,16,512]{3,2,1,0:T(8,128)} %copy-done.2, f32[8,16,512]{2,1,0:T(8,128)S(1)} %get-tuple-element.213.phi_ref, ...), custom_call_target="tpu_custom_call" | custom-call | tf_op jit(solution)/shard_map/cond/branch_1_fun/bulk/pallas_call | solution.py:835
  53.0 0.0 collective-permute-done.13.joint
  53.0 0.8 %joint_fill.10 = (f32[19,8,16,512]{3,2,1,0:T(8,128)}, f32[19,8,16,512]{3,2,1,0:T(8,128)}) custom-call(f32[10,16,512]{2,1,0:T(8,128)S(1)} %collective-permute-done.13.joint, f32[19,8,16,512]{3,2,1,0:T(8,128)} %get-tuple-element.232.f_in, f32[19,8,16,512]{3,2,1,0:T(8,128)} %get-tuple-element.233.g_in), custom_call_target="tpu_custom_call", output_to_operand_aliasing={{0}: (1, {}), {1}: (2, {})} | custom-call | tf_op jit(solution)/shard_map/cond/branch_1_fun/joint_fill/pallas_call | solution.py:848
  53.8 0.0 collective-permute-done.11.across_short
  53.9 0.0 collective-permute-done.9.direct_short
  53.9 5.5 %collective-permute-done.8.direct = f32[10,16,512]{2,1,0:T(8,128)S(1)} collective-permute-done((f32[10,16,512]{2,1,0:T(8,128)S(1)}, f32[10,16,512]{2,1,0:T(8,128)S(1)}, u32[]{:S(2)}, u32[]{:S(2)}) %collective-permute-start.8) | collective-permute-done | bytes 327712 | tf_op jit(solution)/shard_map/cond/branch_1_fun/ppermute | solution.py:785
  59.4 0.0 collective-permute-done.10.across
  59.4 0.8 %merge_fill.10 = (f32[19,8,16,512]{3,2,1,0:T(8,128)}, f32[19,8,16,512]{3,2,1,0:T(8,128)}) custom-call(f32[10,16,512]{2,1,0:T(8,128)S(1)} %collective-permute-done.8.direct, f32[112,512]{1,0:T(8,128)S(1)} %collective-permute-done.9.direct_short, f32[10,16,512]{2,1,0:T(8,128)S(1)} %collective-permute-done.10.across, ...), custom_call_target="tpu_custom_call", output_to_operand_aliasing={{0}: (4, {}), {1}: (5, {})} | custom-call | tf_op jit(solution)/shard_map/cond/branch_1_fun/merge_fill/pallas_call | solution.py:859
  (7 shorter events, 0.1 us)
Async XLA Ops:
  0.6 7.6 %copy-start.1 = (f32[19,8,16,512]{3,2,1,0:T(8,128)S(1)}, f32[19,8,16,512]{3,2,1,0:T(8,128)}, u32[]{:S(2)}) copy-start(f32[19,8,16,512]{3,2,1,0:T(8,128)} %g_ref.5) | copy-start | bytes 14942212
  2.2 8.2 %collective-permute-start.64 = (f32[16,512]{1,0:T(8,128)S(1)}, f32[16,512]{1,0:T(8,128)S(1)}, u32[]{:S(2)}, u32[]{:S(2)}) collective-permute-start(f32[16,512]{1,0:T(8,128)S(1)} %get-tuple-element.466.top), channel_id=1, source_target_pairs={{0,12},{1,13},{2,14},{3,15},{4,8},{5,9},{6,10},{7,11},{8,20},{9,21... | collective-permute-start | bytes 98312 | tf_op jit(solution)/shard_map/ppermute | solution.py:703
  7.2 5.7 %collective-permute-start.63 = (f32[16,512]{1,0:T(8,128)S(1)}, f32[16,512]{1,0:T(8,128)S(1)}, u32[]{:S(2)}, u32[]{:S(2)}) collective-permute-start(f32[16,512]{1,0:T(8,128)S(1)} %get-tuple-element.467.bottom), channel_id=1, source_target_pairs={{0,28},{1,29},{2,30},{3,31},{4,24},{5,25},{6,26},{7,27},{8,4},{9,5... | collective-permute-start | bytes 98312 | tf_op jit(solution)/shard_map/ppermute | solution.py:703
  8.2 6.7 %slice-start = ((s8[4980736]{0:T(1024)(128)(4,1)}), s8[4194304]{0:T(1024)(128)(4,1)S(1)}, s32[]{:S(2)}) async-start(s8[4980736]{0:T(1024)(128)(4,1)} %bitcast.1), calls=%async_computation | async-start | bytes 8388608
  8.2 4.8 %copy-start = (s32[4]{0:T(128)S(1)}, s32[4]{0:T(128)}, u32[]{:S(2)}) copy-start(s32[4]{0:T(128)} %offsets.1) | copy-start | bytes 52
  8.2 6.7 %slice-start.1 = ((s8[4980736]{0:T(1024)(128)(4,1)}), s8[786432]{0:T(1024)(128)(4,1)S(1)}, s32[]{:S(2)}) async-start(s8[4980736]{0:T(1024)(128)(4,1)} %bitcast.1), calls=%async_computation.1 | async-start | bytes 1572864
  10.4 5.5 %collective-permute-start.66 = (f32[40,512]{1,0:T(8,128)S(1)}, f32[40,512]{1,0:T(8,128)S(1)}, u32[]{:S(2)}, u32[]{:S(2)}) collective-permute-start(f32[40,512]{1,0:T(8,128)S(1)} %constant_dynamic-update-slice_fusion.2.after_south), channel_id=1, source_target_pairs={{0,7},{1,0},{2,1},{3,2},{4,3},{5,4},{6,5},{7,6},{8,15},{9,8},{10,9... | collective-permute-start | bytes 245768 | tf_op jit(solution)/shard_map/ppermute | solution.py:703
  12.9 5.7 %collective-permute-start.65 = (f32[40,512]{1,0:T(8,128)S(1)}, f32[40,512]{1,0:T(8,128)S(1)}, u32[]{:S(2)}, u32[]{:S(2)}) collective-permute-start(f32[40,512]{1,0:T(8,128)S(1)} %constant_dynamic-update-slice_fusion.after_north), channel_id=1, source_target_pairs={{0,1},{1,2},{2,3},{3,4},{4,5},{5,6},{6,7},{7,0},{8,9},{9,10},{10,1... | collective-permute-start | bytes 245768 | tf_op jit(solution)/shard_map/ppermute | solution.py:703
  18.6 3.5 %copy-start.2 = (f32[19,8,16,512]{3,2,1,0:T(8,128)}, f32[19,8,16,512]{3,2,1,0:T(8,128)S(1)}, u32[]{:S(2)}) copy-start(f32[19,8,16,512]{3,2,1,0:T(8,128)S(1)} %get-tuple-element.210.g_ref) | copy-start | bytes 14942212 | tf_op jit(solution)/shard_map/cond
  20.2 1.9 %collective-permute-start.12 = (f32[10,24,512]{2,1,0:T(8,128)S(1)}, f32[10,24,512]{2,1,0:T(8,128)S(1)}, u32[]{:S(2)}, u32[]{:S(2)}) collective-permute-start(f32[10,24,512]{2,1,0:T(8,128)S(1)} %get-tuple-element.228), channel_id=1, source_target_pairs={{0,1},{1,0},{2,3},{3,2},{4,5},{5,4},{6,7},{7,6},{8,9},{9,8},{10,11... | collective-permute-start | bytes 1474568 | tf_op jit(solution)/shard_map/cond/branch_1_fun/ppermute | solution.py:703
  20.2 6.7 %collective-permute-start.7 = (f32[10,8,512]{2,1,0:T(8,128)S(1)}, f32[10,8,512]{2,1,0:T(8,128)S(1)}, u32[]{:S(2)}, u32[]{:S(2)}) collective-permute-start(f32[10,8,512]{2,1,0:T(8,128)S(1)} %get-tuple-element.222), channel_id=1, source_target_pairs={{0,7},{1,2},{2,1},{3,4},{4,3},{5,6},{6,5},{7,0},{8,15},{9,10},{10,... | collective-permute-start | bytes 491528 | tf_op jit(solution)/shard_map/cond/branch_1_fun/ppermute | solution.py:703
  22.1 30.9 %collective-permute-start.13 = (f32[10,16,512]{2,1,0:T(8,128)S(1)}, f32[10,16,512]{2,1,0:T(8,128)S(1)}, u32[]{:S(2)}, u32[]{:S(2)}) collective-permute-start(f32[10,16,512]{2,1,0:T(8,128)S(1)} %slice_add_fusion.1.after), channel_id=1, source_target_pairs={{0,12},{1,29},{2,14},{3,31},{4,8},{5,25},{6,10},{7,27},{8,20},{9,5... | collective-permute-start | bytes 983048 | tf_op jit(solution)/shard_map/cond/branch_1_fun/ppermute | solution.py:703
  27.0 32.4 %collective-permute-start.8 = (f32[10,16,512]{2,1,0:T(8,128)S(1)}, f32[10,16,512]{2,1,0:T(8,128)S(1)}, u32[]{:S(2)}, u32[]{:S(2)}) collective-permute-start(f32[10,16,512]{2,1,0:T(8,128)S(1)} %get-tuple-element.223), channel_id=1, source_target_pairs={{0,28},{1,13},{2,30},{3,15},{4,24},{5,9},{6,26},{7,11},{8,4},{10,6... | collective-permute-start | bytes 983048 | tf_op jit(solution)/shard_map/cond/branch_1_fun/ppermute | solution.py:785
  28.9 30.5 %collective-permute-start.10 = (f32[10,16,512]{2,1,0:T(8,128)S(1)}, f32[10,16,512]{2,1,0:T(8,128)S(1)}, u32[]{:S(2)}, u32[]{:S(2)}) collective-permute-start(f32[10,16,512]{2,1,0:T(8,128)S(1)} %get-tuple-element.225), channel_id=1, source_target_pairs={{8,19},{10,21},{12,23},{14,17},{16,27},{17,14},{18,29},{19,8},{20,... | collective-permute-start | bytes 983048 | tf_op jit(solution)/shard_map/cond/branch_1_fun/ppermute | solution.py:785
  29.6 24.3 %collective-permute-start.9 = (f32[112,512]{1,0:T(8,128)S(1)}, f32[112,512]{1,0:T(8,128)S(1)}, u32[]{:S(2)}, u32[]{:S(2)}) collective-permute-start(f32[112,512]{1,0:T(8,128)S(1)} %get-tuple-element.224), channel_id=1, source_target_pairs={{9,21},{11,23},{13,17},{15,19},{16,12},{17,29},{18,14},{19,31},{20... | collective-permute-start | bytes 688136 | tf_op jit(solution)/shard_map/cond/branch_1_fun/ppermute | solution.py:785
  30.2 23.6 %collective-permute-start.11 = (f32[72,512]{1,0:T(8,128)S(1)}, f32[72,512]{1,0:T(8,128)S(1)}, u32[]{:S(2)}, u32[]{:S(2)}) collective-permute-start(f32[72,512]{1,0:T(8,128)S(1)} %get-tuple-element.226), channel_id=1, source_target_pairs={{0,11},{1,30},{2,13},{3,24},{4,15},{5,26},{6,9},{7,28},{9,6},{11,0... | collective-permute-start | bytes 442376 | tf_op jit(solution)/shard_map/cond/branch_1_fun/ppermute | solution.py:785
